TPU v7x, 128 devices: a whole 4x4x4 slice. The times are simulated.
128 devices in a mesh: car: 8 (over z_hi, x), dom: 16 (over y, z_lo, core).
Axes of the slice: x: 4, y: 4, z: 4 (z_hi: 2, z_lo: 2; z = z_hi * 2 + z_lo), core: 2. Of those that a mesh axis runs over, the one named last changes fastest.
Arguments:
- points: bfloat16 [131072, 768], P(('car', 'dom')), parts along dimension 0, may hold values from -6 to 6
- norm_gain: float32 [768], replicated, may hold values from 0.25 to 1.75
- w_qkv: bfloat16 [768, 2304], replicated, may hold values from -0.12629537 to 0.12629537
- w_out: bfloat16 [768, 768], replicated, may hold values from -0.75 to 0.75
- w_cross_q: bfloat16 [768, 768], replicated, may hold values from -0.12629537 to 0.12629537
- w_cross_kv: bfloat16 [768, 1536], replicated, may hold values from -0.12629537 to 0.12629537
- w_cross_out: bfloat16 [768, 768], replicated, may hold values from -0.75 to 0.75
- live_blocks: int32 [128], P(('car', 'dom')), parts along dimension 0, may hold values from 4 to 8, as said below
- send_blocks: int32 [512], P(('car', 'dom')), parts along dimension 0, may hold values from 0 to 7, as said below
- neighbours: int32 [1024, 8], P(('car', 'dom')), parts along dimension 0, may hold values from 0 to 11, as said below
- neighbour_count: int32 [1024], P(('car', 'dom')), parts along dimension 0, may hold values from 2 to 8
- anchor_index: int32 [32768], P(('car', 'dom')), parts along dimension 0, may hold values from 0 to 1023, as said below
Outputs:
- mixed: bfloat16 [131072, 768], P(('car', 'dom')), parts along dimension 0
There are 8 independent parts, one for each index of `car`. A program takes and returns all parts, laid end to end along the dimension named above; an argument that names none is the same for every part. Nothing has to cross between parts.
Inputs may be any that keep to these rules, and one draw needn't show every extreme that they name: `live_blocks`: some partition of every car has all 8 blocks live. `send_blocks`: the 2 blocks of each list are distinct live blocks of the sending partition. `neighbours`: slot 0 of every block is the block itself; the first partition of a car names no block of a previous one and the last none of a next one; counted slots of a live block name live blocks. `anchor_index`: anchors lie in live blocks of their partition.
All inputs are finite; a program needn't handle non-finite values.
Results may differ from a plain program's by a relative error of at most 0.0086.
Values may be sent and summed in bfloat16 or wider, within the bound.
No kernel may reach another device: no remote copies, remote signals or barrier semaphores. Data moves between devices by JAX's collectives and lax.ppermute only.
A program may use at most 256 MiB of HBM per device.

v0:
```python
import functools

import jax
import jax.numpy as jnp
from jax import lax
from jax.experimental import pallas as pl
from jax.experimental.pallas import tpu as pltpu
from jax.sharding import PartitionSpec as P

HEADS = 12
BLK = 128
HB = 2
PAIR = 128
HALF = 64
CHUNK = 512
SCALE = HALF**-0.5 * 1.4426950408889634
LIMIT = 32 * 2**20
WIDE = 61 * 2**20
NEG = -1e30
F32 = jnp.float32
BF16 = jnp.bfloat16


def params(limit=LIMIT):
    return pltpu.CompilerParams(vmem_limit_bytes=limit)


def cost(flops, nbytes, trans=0):
    return pl.CostEstimate(flops=int(flops), bytes_accessed=int(nbytes), transcendentals=int(trans))


def struct(rows, cols, dtype=BF16):
    return jax.ShapeDtypeStruct((rows, cols), dtype)


def whole(array):
    return pl.BlockSpec(array.shape, lambda *_: (0,) * array.ndim)


def mm(a, b):
    return jnp.dot(a, b, preferred_element_type=F32)


def mm_t(a, b):
    return lax.dot_general(a, b, (((1,), (1,)), ((), ())), preferred_element_type=F32)


def normed_rows(rows, gain):
    floats = rows.astype(F32)
    factor = lax.rsqrt(jnp.mean(floats * floats, axis=-1, keepdims=True) + 1e-06)
    return (floats * factor * gain).astype(BF16)


def pick_kernel(
    send_ref, index_ref, gain_ref, source_ref, anchor_ref, prev_ref, next_ref, points_ref, sem
):
    copy = pltpu.make_async_copy(source_ref, points_ref, sem)
    copy.start()
    rows = points_ref.shape[0]
    anchors = index_ref.shape[1]
    slot = lax.broadcasted_iota(jnp.int32, (rows, anchors), 0)
    chosen = jnp.where(slot == index_ref[...], 1.0, 0.0).astype(BF16)
    copy.wait()
    picked = lax.dot_general(
        chosen, points_ref[...], (((0,), (0,)), ((), ())), preferred_element_type=F32
    )
    anchor_ref[...] = normed_rows(picked, gain_ref[...])
    for place in range(HB):
        for base, out_ref in ((0, prev_ref), (HB, next_ref)):
            start = pl.multiple_of(send_ref[base + place] * BLK, BLK)
            out_ref[place * BLK : (place + 1) * BLK, :] = normed_rows(
                points_ref[pl.ds(start, BLK), :], gain_ref[...]
            )


def pick(points, gain, send_blocks, anchor_index):
    rows, width = points.shape
    anchors = anchor_index.shape[0]
    index = anchor_index.reshape(1, anchors)
    own = struct(anchors, width)
    side = struct(HB * BLK, width)
    vmem = pl.BlockSpec(memory_space=pltpu.VMEM)
    return pl.pallas_call(
        pick_kernel,
        out_shape=(own, side, side),
        in_specs=[
            pl.BlockSpec(memory_space=pltpu.SMEM),
            vmem,
            vmem,
            pl.BlockSpec(memory_space=pltpu.HBM),
        ],
        scratch_shapes=[pltpu.VMEM((rows, width), BF16), pltpu.SemaphoreType.DMA],
        compiler_params=params(WIDE),
        cost_estimate=cost(2 * anchors * rows * width, 4 * rows * width),
    )(send_blocks, index, gain, points)


def project_kernel(points_ref, gain_ref, wqkv_ref, wcq_ref, out_ref, normed_ref):
    rows, width = points_ref.shape
    tile = rows // 4
    for at in range(0, rows, tile):
        normed = normed_rows(points_ref[at : at + tile, :], gain_ref[...])
        normed_ref[at : at + tile, :] = normed
        out_ref[at : at + tile, :width] = (mm(normed, wqkv_ref[:, :width]) * SCALE).astype(BF16)
    for at in range(width, 3 * width, width):
        out_ref[:, at : at + width] = mm(normed_ref[...], wqkv_ref[:, at : at + width]).astype(BF16)
    out_ref[:, 3 * width :] = (mm(normed_ref[...], wcq_ref[...]) * SCALE).astype(BF16)


def project(points, gain, w_qkv, w_cross_q):
    rows, width = points.shape
    vmem = pl.BlockSpec(memory_space=pltpu.VMEM)
    return pl.pallas_call(
        project_kernel,
        out_shape=struct(rows, 4 * width),
        in_specs=[vmem] * 4,
        out_specs=vmem,
        scratch_shapes=[pltpu.VMEM((rows, width), BF16)],
        compiler_params=params(24 * 2**20),
        cost_estimate=cost(2 * rows * width * 4 * width, 20 * rows * width),
    )(points, gain, w_qkv, w_cross_q)


def split_heads(rows):
    lane = lax.broadcasted_iota(jnp.int32, rows.shape, 1)
    zero = jnp.zeros_like(rows)
    return jnp.concatenate(
        [jnp.where(lane < HALF, rows, zero), jnp.where(lane >= HALF, rows, zero)], axis=0
    )


def join_heads(both):
    count = both.shape[0] // 2
    lane = lax.broadcasted_iota(jnp.int32, (count, PAIR), 1)
    return jnp.where(lane < HALF, both[:count], both[count:])


def weigh(weights, values):
    weights = weights.astype(BF16)
    count = weights.shape[0] // 2
    lane = lax.broadcasted_iota(jnp.int32, values.shape, 1)
    one = jnp.ones_like(values)
    return jnp.concatenate(
        [
            mm(weights[:count], jnp.where(lane < HALF, values, one)),
            mm(weights[count:], jnp.where(lane < HALF, one, values)),
        ],
        axis=0,
    )


def weigh_wide(weights, values):
    ones = jnp.ones((values.shape[0], PAIR), BF16)
    return mm(weights.astype(BF16), jnp.concatenate([values, ones], axis=1))


def block_kernel(
    ids_ref,
    count_ref,
    live_ref,
    projected_ref,
    low_ref,
    high_ref,
    weight_ref,
    out_ref,
    table_ref,
):
    block = pl.program_id(0)
    slots = ids_ref.shape[1]
    blocks = count_ref.shape[0]
    width = low_ref.shape[1]

    @pl.when(block == 0)
    def _():
        normed = jnp.concatenate([low_ref[...], high_ref[...]], axis=0)
        for n in range(2):
            table_ref[n] = mm(normed, weight_ref[:, (1 + n) * width : (2 + n) * width]).astype(BF16)

    count = count_ref[block]
    pairs = jnp.where(block < live_ref[0], (count + 1) // 2, 0)

    @pl.when(pairs == 0)
    def _():
        out_ref[...] = jnp.zeros_like(out_ref)

    for used in range(1, slots // 2 + 1):

        @pl.when(pairs == used)
        def _(used=used):
            places = []
            for n in range(2 * used):
                place = ids_ref[block, n]
                own = pl.multiple_of(jnp.minimum(place, blocks - 1) * BLK, BLK)
                received = pl.multiple_of(jnp.maximum(place - blocks, 0) * BLK, BLK)
                places.append((place < blocks, own, received))
            dropped = jnp.where(count == 2 * used, 0.0, NEG)
            here = pl.ds(pl.multiple_of(block * BLK, BLK), BLK)

            def rows_of(which, part, at):
                lanes = slice((1 + which) * width + at, (1 + which) * width + at + PAIR)
                return jnp.concatenate(
                    [
                        jnp.where(
                            is_own,
                            projected_ref[pl.ds(own, BLK), lanes],
                            table_ref[which, pl.ds(received, BLK), at : at + PAIR],
                        )
                        for is_own, own, received in places[2 * part : 2 * part + 2]
                    ],
                    axis=0,
                )

            for at in range(0, width, PAIR):
                query = split_heads(projected_ref[here, at : at + PAIR])
                scores = [mm_t(query, rows_of(0, part, at)) for part in range(used)]
                last = scores[-1]
                scores[-1] = jnp.concatenate([last[:, :BLK], last[:, BLK:] + dropped], axis=1)
                top = functools.reduce(jnp.maximum, scores)
                top = jnp.max(top, axis=1, keepdims=True)
                total = sum(
                    weigh_wide(jnp.exp2(scores[part] - top), rows_of(1, part, at))
                    for part in range(used)
                )
                out_ref[:, at : at + PAIR] = join_heads(total[:, :PAIR] / total[:, PAIR:]).astype(
                    BF16
                )


def block_attention(projected, low, high, w_qkv, ids, counts, live):
    rows = projected.shape[0]
    width = low.shape[1]
    side = low.shape[0]
    blocks = rows // BLK
    vmem = pl.BlockSpec(memory_space=pltpu.VMEM)
    return pl.pallas_call(
        block_kernel,
        out_shape=struct(rows, width),
        grid_spec=pltpu.PrefetchScalarGridSpec(
            num_scalar_prefetch=3,
            grid=(blocks,),
            in_specs=[vmem] * 4,
            out_specs=pl.BlockSpec((BLK, width), lambda i, *_: (i, 0)),
            scratch_shapes=[pltpu.VMEM((2, 2 * side, width), BF16)],
        ),
        compiler_params=params(),
        cost_estimate=cost(16 * rows * 5 * BLK * width, 12 * rows * width, rows * 5 * BLK * 12),
    )(ids, counts, live, projected, low, high, w_qkv)


def anchor_kernel(count, *refs):
    parts = refs[:count]
    weight_ref, out_ref, held_ref, sems = refs[count:]
    rows, width = parts[0].shape
    group = count // 2
    stores = []
    for first in range(0, count, group):
        normed = jnp.concatenate([part[...] for part in parts[first : first + group]], axis=0)
        for n in range(2):
            columns = slice(n * width, (n + 1) * width)
            slot = len(stores)
            held_ref[slot] = mm(normed, weight_ref[:, columns]).astype(BF16)
            store = pltpu.make_async_copy(
                held_ref.at[slot],
                out_ref.at[first * rows : (first + group) * rows, columns],
                sems.at[slot],
            )
            store.start()
            stores.append(store)
    for store in stores:
        store.wait()


def anchor_project(parts, weight):
    rows, width = parts[0].shape
    every = len(parts) * rows
    vmem = pl.BlockSpec(memory_space=pltpu.VMEM)
    return pl.pallas_call(
        functools.partial(anchor_kernel, len(parts)),
        out_shape=struct(every, 2 * width),
        in_specs=[vmem] * (len(parts) + 1),
        out_specs=pl.BlockSpec(memory_space=pltpu.HBM),
        scratch_shapes=[
            pltpu.VMEM((4, every // 2, width), BF16),
            pltpu.SemaphoreType.DMA((4,)),
        ],
        compiler_params=params(),
        cost_estimate=cost(4 * every * width * width, 6 * every * width),
    )(*parts, weight)


def sweep(query, keys_ref, values_ref):
    top, total = None, None
    for start in range(0, keys_ref.shape[0], CHUNK):
        scores = mm_t(query, keys_ref[start : start + CHUNK, :])
        values = values_ref[start : start + CHUNK, :]
        here = jnp.max(scores, axis=1, keepdims=True)
        if top is None:
            top = here
            total = weigh(jnp.exp2(scores - top), values)
        else:
            later = jnp.maximum(top, here)
            total = total * jnp.exp2(top - later) + weigh(jnp.exp2(scores - later), values)
            top = later
    sums = pltpu.roll(total, HALF, 1)
    return join_heads(total / sums), join_heads(top + jnp.log2(sums))


def cross_kernel(queries_ref, keys_ref, values_ref, mean_ref, size_ref):
    query = split_heads(queries_ref[...])
    mean_ref[...], size_ref[...] = sweep(query, keys_ref, values_ref)


def cross_part(projected, anchor_kv):
    rows = projected.shape[0]
    width = projected.shape[1] // 4
    count = anchor_kv.shape[0]
    pairs = width // PAIR
    tile = rows
    state = struct(rows, width, F32)
    spec = pl.BlockSpec((tile, PAIR), lambda h, i: (i, h))
    return pl.pallas_call(
        cross_kernel,
        out_shape=(state, state),
        grid=(pairs, rows // tile),
        in_specs=[
            pl.BlockSpec((tile, PAIR), lambda h, i: (i, 3 * pairs + h)),
            pl.BlockSpec((count, PAIR), lambda h, i: (0, h)),
            pl.BlockSpec((count, PAIR), lambda h, i: (0, pairs + h)),
        ],
        out_specs=[spec, spec],
        compiler_params=params(WIDE),
        cost_estimate=cost(16 * rows * count * width, 20 * rows * width, 12 * rows * count),
    )(projected, anchor_kv, anchor_kv)


def final_kernel(
    live_ref,
    queries_ref,
    keys_ref,
    values_ref,
    mean_ref,
    size_ref,
    block_source_ref,
    wout_source_ref,
    wcross_source_ref,
    out_ref,
    held_ref,
    block_ref,
    wout_ref,
    wcross_ref,
    sems,
):
    pair = pl.program_id(0)
    rows = queries_ref.shape[0]
    fetches = [
        pltpu.make_async_copy(source, target, sems.at[n])
        for n, (source, target) in enumerate(
            [
                (block_source_ref, block_ref),
                (wout_source_ref, wout_ref),
                (wcross_source_ref, wcross_ref),
            ]
        )
    ]

    @pl.when(pair == 0)
    def _():
        for fetch in fetches:
            fetch.start()

    query = split_heads(queries_ref[...])
    mean, size = sweep(query, keys_ref, values_ref)
    top = jnp.maximum(size, size_ref[...])
    share, other = jnp.exp2(size - top), jnp.exp2(size_ref[...] - top)
    held_ref[pair] = ((mean * share + mean_ref[...] * other) / (share + other)).astype(BF16)

    @pl.when(pair == pl.num_programs(0) - 1)
    def _():
        for fetch in fetches:
            fetch.wait()
        cross = jnp.concatenate([held_ref[n] for n in range(held_ref.shape[0])], axis=1)
        mixed = mm(block_ref[...], wout_ref[...]) + mm(cross, wcross_ref[...])
        place = lax.broadcasted_iota(jnp.int32, (rows, 1), 0)
        out_ref[...] = jnp.where(place // BLK < live_ref[0], mixed, 0.0).astype(BF16)


def finish(projected, anchor_kv, state, block_attn, w_out, w_cross_out, live):
    rows = projected.shape[0]
    width = projected.shape[1] // 4
    count = anchor_kv.shape[0]
    pairs = width // PAIR
    spec = pl.BlockSpec((rows, PAIR), lambda h, *_: (0, h))
    hbm = pl.BlockSpec(memory_space=pltpu.HBM)
    return pl.pallas_call(
        final_kernel,
        out_shape=struct(rows, width),
        grid_spec=pltpu.PrefetchScalarGridSpec(
            num_scalar_prefetch=1,
            grid=(pairs,),
            in_specs=[
                pl.BlockSpec((rows, PAIR), lambda h, *_: (0, 3 * pairs + h)),
                pl.BlockSpec((count, PAIR), lambda h, *_: (0, h)),
                pl.BlockSpec((count, PAIR), lambda h, *_: (0, pairs + h)),
                spec,
                spec,
                hbm,
                hbm,
                hbm,
            ],
            out_specs=pl.BlockSpec((rows, width), lambda h, *_: (0, 0)),
            scratch_shapes=[
                pltpu.VMEM((pairs, rows, PAIR), BF16),
                pltpu.VMEM((rows, width), BF16),
                pltpu.VMEM((width, width), BF16),
                pltpu.VMEM((width, width), BF16),
                pltpu.SemaphoreType.DMA((3,)),
            ],
        ),
        compiler_params=params(WIDE),
        cost_estimate=cost(16 * rows * count * width, 28 * rows * width, 12 * rows * count),
    )(live, projected, anchor_kv, anchor_kv, *state, block_attn, w_out, w_cross_out)


def after(*arrays):
    return lax.optimization_barrier(arrays)


def permute(array, target):
    size = lax.axis_size("dom")
    pairs = [(i, target(i)) for i in range(size) if 0 <= target(i) < size]
    return lax.ppermute(array, "dom", pairs)


def local(
    points,
    norm_gain,
    w_qkv,
    w_out,
    w_cross_q,
    w_cross_kv,
    w_cross_out,
    live_blocks,
    send_blocks,
    neighbours,
    neighbour_count,
    anchor_index,
):
    rows, width = points.shape
    size = lax.axis_size("dom")
    column, ring = 2, 4
    anchors, to_prev, to_next = pick(points, norm_gain, send_blocks, anchor_index)

    def around(array):
        return [permute(array, lambda i, n=n: (i + n * ring) % size) for n in (1, -1, 2)]

    beside = permute(anchors, lambda i: i ^ column)
    low = permute(to_next, lambda i: i + 1)
    high = permute(to_prev, lambda i: i - 1)
    rows_here = around(anchors)
    points, anchors = after(points, anchors)
    projected = project(points, norm_gain, w_qkv, w_cross_q)
    beside, rows_here[0], rows_here[1], projected = after(
        beside, rows_here[0], rows_here[1], projected
    )
    rows_beside = [permute(rows_here[n], lambda i: i ^ column) for n in range(2)]
    rows_beside.append(permute(beside, lambda i: (i + 2 * ring) % size))
    block_attn = block_attention(
        projected, low, high, w_qkv, neighbours, neighbour_count, live_blocks
    )
    *parts, block_attn = after(anchors, beside, *rows_here, *rows_beside, block_attn)
    kv_own = anchor_project(parts, w_cross_kv)
    kv_other = permute(kv_own, lambda i: i ^ 1)
    state = cross_part(projected, kv_own)
    return finish(projected, kv_other, state, block_attn, w_out, w_cross_out, live_blocks)


def solution(mesh):
    sharded = P(("car", "dom"))
    in_specs = (
        P(("car", "dom"), None),
        P(),
        P(),
        P(),
        P(),
        P(),
        P(),
        sharded,
        sharded,
        P(("car", "dom"), None),
        sharded,
        sharded,
    )
    out_specs = P(("car", "dom"), None)
    return jax.shard_map(local, mesh=mesh, in_specs=in_specs, out_specs=out_specs, check_vma=False)
```

profile of v0, /device:TPU:23, one launch (start us, length us, event | category | flops | bytes accessed | tf_op | source)
XLA Modules:
  0.0 126.9 jit_solution(8943849475650702949)
XLA Ops:
  0.0 3.8 %shard_map.118 = (bf16[256,768]{1,0:T(8,128)(2,1)}, bf16[256,768]{1,0:T(8,128)(2,1)}, bf16[256,768]{1,0:T(8,128)(2,1)}) custom-call(s32[4]{0:T(128)} %send_ref.1, s32[1,256]{1,0:T(1,128)} %bitcast.1, f32[768]{0:T(1024)} %gain_ref.3, bf16[1024,768]{1,0:T(8,128)(2,1)} %points_ref), custom_call_target="tpu_custom_call" | custom-call | flops 402653184 | bytes 3145728 | tf_op jit(solution)/shard_map/pallas_call | solution.py:83
  3.8 1.7 %collective-permute-start = (bf16[256,768]{1,0:T(8,128)(2,1)}, bf16[256,768]{1,0:T(8,128)(2,1)S(1)}, u32[]{:S(2)}, u32[]{:S(2)}) collective-permute-start(bf16[256,768]{1,0:T(8,128)(2,1)} %get-tuple-element.34.refs_0_), channel_id=1, source_target_pairs={{0,2},{1,3},{2,0},{3,1},{4,6},{5,7},{6,4},{7,5},{8,10},{9,11},{10,... | collective-permute-start | bytes 1179656 | tf_op jit(solution)/shard_map/ppermute | solution.py:431
  5.6 1.0 collective-permute-start.1
  6.6 0.5 collective-permute-start.2
  7.0 3.1 %collective-permute-start.7 = (bf16[256,768]{1,0:T(8,128)(2,1)}, bf16[256,768]{1,0:T(8,128)(2,1)S(1)}, u32[]{:S(2)}, u32[]{:S(2)}) collective-permute-start(bf16[256,768]{1,0:T(8,128)(2,1)} %get-tuple-element.32), channel_id=1, source_target_pairs={{0,1},{1,2},{2,3},{3,4},{4,5},{5,6},{6,7},{7,8},{8,9},{9,10},{10,1... | collective-permute-start | bytes 1179656 | tf_op jit(solution)/shard_map/ppermute | solution.py:431
  10.2 2.2 %collective-permute-start.8 = (bf16[256,768]{1,0:T(8,128)(2,1)}, bf16[256,768]{1,0:T(8,128)(2,1)S(1)}, u32[]{:S(2)}, u32[]{:S(2)}) collective-permute-start(bf16[256,768]{1,0:T(8,128)(2,1)} %get-tuple-element.33), channel_id=1, source_target_pairs={{1,0},{2,1},{3,2},{4,3},{5,4},{6,5},{7,6},{8,7},{9,8},{10,9},{11,1... | collective-permute-start | bytes 1179656 | tf_op jit(solution)/shard_map/ppermute | solution.py:431
  13.0 0.0 copy-start
  13.0 1.4 %copy-done = bf16[1024,768]{1,0:T(8,128)(2,1)S(1)} copy-done((bf16[1024,768]{1,0:T(8,128)(2,1)S(1)}, bf16[1024,768]{1,0:T(8,128)(2,1)}, u32[]{:S(2)}) %copy-start) | copy-done | bytes 1572888
  14.4 0.7 copy-done.1
  15.1 2.0 %copy-done.2 = bf16[768,2304]{1,0:T(8,128)(2,1)S(1)} copy-done((bf16[768,2304]{1,0:T(8,128)(2,1)S(1)}, bf16[768,2304]{1,0:T(8,128)(2,1)}, u32[]{:S(2)}) %copy-start.2) | copy-done | bytes 3538968
  17.1 1.3 copy-done.5
  18.4 5.2 %shard_map.119.projected_ref.queries_ref = bf16[1024,3072]{1,0:T(8,128)(2,1)S(1)} custom-call(bf16[1024,768]{1,0:T(8,128)(2,1)S(1)} %copy-done, f32[768]{0:T(1024)S(1)} %copy-done.1, bf16[768,2304]{1,0:T(8,128)(2,1)S(1)} %copy-done.2, bf16[768,768]{1,0:T(8,128)(2,1)S(1)} %copy-done.5), custom_call_target="tpu_custom_call" | custom-call | flops 4831838208 | bytes 15728640 | tf_op jit(solution)/shard_map/pallas_call | solution.py:113
  23.7 0.0 copy-start.4
  23.7 1.1 collective-permute-start.3
  24.7 0.0 collective-permute-done.1.refs_2_
  24.8 1.4 %collective-permute-start.4 = (bf16[256,768]{1,0:T(8,128)(2,1)S(1)}, bf16[256,768]{1,0:T(8,128)(2,1)S(1)}, u32[]{:S(2)}, u32[]{:S(2)}) collective-permute-start(bf16[256,768]{1,0:T(8,128)(2,1)S(1)} %collective-permute-done.1.refs_2_), channel_id=1, source_target_pairs={{0,2},{1,3},{2,0},{3,1},{4,6},{5,7},{6,4},{7,5},{8,10},{9,11},{10,... | collective-permute-start | bytes 1179656 | tf_op jit(solution)/shard_map/ppermute | solution.py:431
  26.2 0.1 collective-permute-start.5
  26.3 2.6 %collective-permute-start.6 = (bf16[256,768]{1,0:T(8,128)(2,1)S(1)}, bf16[256,768]{1,0:T(8,128)(2,1)S(1)}, u32[]{:S(2)}, u32[]{:S(2)}) collective-permute-start(bf16[256,768]{1,0:T(8,128)(2,1)S(1)} %collective-permute-done.refs_1_), channel_id=1, source_target_pairs={{0,8},{1,9},{2,10},{3,11},{4,12},{5,13},{6,14},{7,15},{8,0},{9,1},... | collective-permute-start | bytes 1179656 | tf_op jit(solution)/shard_map/ppermute | solution.py:431
  28.9 13.1 %shard_map.120.block_source_ref = bf16[1024,768]{1,0:T(8,128)(2,1)S(1)} custom-call(s32[8,8]{1,0:T(8,128)S(1)} %copy-done.7, s32[8]{0:T(128)S(1)} %copy-done.8, s32[1]{0:T(128)S(6)} %copy.13.live_ref, bf16[1024,3072]{1,0:T(8,128)(2,1)S(1)} %shard_map.119.projected_ref.queries_ref, bf16[256,768]{1,0:T(8,128)(2,1)S(1)} %collective-permute-done.7.low_ref, ...), custom_call_target="tpu_custom_call" | custom-call | flops 8053063680 | bytes 9437184 | tf_op jit(solution)/shard_map/pallas_call | solution.py:235
  42.1 0.3 collective-permute-done.5.refs_6_
  42.4 6.4 %shard_map.121.keys_ref.values_ref = bf16[2048,1536]{1,0:T(8,128)(2,1)} custom-call(bf16[256,768]{1,0:T(8,128)(2,1)S(1)} %copy-done.6, bf16[256,768]{1,0:T(8,128)(2,1)S(1)} %collective-permute-done.refs_1_, bf16[256,768]{1,0:T(8,128)(2,1)S(1)} %collective-permute-done.1.refs_2_, bf16[256,768]{1,0:T(8,128)(2,1)S(1)} %collective-permute-done.2.refs_3_, ...), custom_call_target="tpu_custom_call" | custom-call | flops 4831838208 | bytes 9437184 | tf_op jit(solution)/shard_map/pallas_call | solution.py:277
  48.8 8.2 %collective-permute-start.9 = (bf16[2048,1536]{1,0:T(8,128)(2,1)}, bf16[2048,1536]{1,0:T(8,128)(2,1)}, u32[]{:S(2)}, u32[]{:S(2)}) collective-permute-start(bf16[2048,1536]{1,0:T(8,128)(2,1)} %shard_map.121.keys_ref.values_ref), channel_id=1, source_target_pairs={{0,1},{1,0},{2,3},{3,2},{4,5},{5,4},{6,7},{7,6},{8,9},{9,8},{10,11... | collective-permute-start | bytes 18874376 | tf_op jit(solution)/shard_map/ppermute | solution.py:431
  57.0 32.7 %shard_map.122 = (f32[1024,768]{1,0:T(8,128)}, f32[1024,768]{1,0:T(8,128)}) custom-call(bf16[1024,3072]{1,0:T(8,128)(2,1)} %copy-done.9, bf16[2048,1536]{1,0:T(8,128)(2,1)} %shard_map.121.keys_ref.values_ref, bf16[2048,1536]{1,0:T(8,128)(2,1)} %shard_map.121.keys_ref.values_ref), custom_call_target="tpu_custom_call" | custom-call | flops 25769803776 | bytes 15728640 | tf_op jit(solution)/shard_map/pallas_call | solution.py:321
  89.7 37.0 %shard_map.123 = bf16[1024,768]{1,0:T(8,128)(2,1)} custom-call(s32[1]{0:T(128)S(6)} %copy.13.live_ref, bf16[1024,3072]{1,0:T(8,128)(2,1)} %copy-done.9, bf16[2048,1536]{1,0:T(8,128)(2,1)} %collective-permute-done.9.keys_ref.values_ref, bf16[2048,1536]{1,0:T(8,128)(2,1)} %collective-permute-done.9.keys_ref.values_ref, ...), custom_call_target="tpu_custom_call" | custom-call | flops 25769803776 | bytes 22020096 | tf_op jit(solution)/shard_map/pallas_call | solution.py:394
  (24 shorter events, 0.1 us)
Async XLA Ops:
  3.8 19.8 %collective-permute-start = (bf16[256,768]{1,0:T(8,128)(2,1)}, bf16[256,768]{1,0:T(8,128)(2,1)S(1)}, u32[]{:S(2)}, u32[]{:S(2)}) collective-permute-start(bf16[256,768]{1,0:T(8,128)(2,1)} %get-tuple-element.34.refs_0_), channel_id=1, source_target_pairs={{0,2},{1,3},{2,0},{3,1},{4,6},{5,7},{6,4},{7,5},{8,10},{9,11},{10,... | collective-permute-start | bytes 1179656 | tf_op jit(solution)/shard_map/ppermute | solution.py:431
  5.6 19.2 %collective-permute-start.1 = (bf16[256,768]{1,0:T(8,128)(2,1)}, bf16[256,768]{1,0:T(8,128)(2,1)S(1)}, u32[]{:S(2)}, u32[]{:S(2)}) collective-permute-start(bf16[256,768]{1,0:T(8,128)(2,1)} %get-tuple-element.34.refs_0_), channel_id=1, source_target_pairs={{0,4},{1,5},{2,6},{3,7},{4,8},{5,9},{6,10},{7,11},{8,12},{9,13},{1... | collective-permute-start | bytes 1179656 | tf_op jit(solution)/shard_map/ppermute | solution.py:431
  6.6 18.2 %collective-permute-start.2 = (bf16[256,768]{1,0:T(8,128)(2,1)}, bf16[256,768]{1,0:T(8,128)(2,1)S(1)}, u32[]{:S(2)}, u32[]{:S(2)}) collective-permute-start(bf16[256,768]{1,0:T(8,128)(2,1)} %get-tuple-element.34.refs_0_), channel_id=1, source_target_pairs={{0,12},{1,13},{2,14},{3,15},{4,0},{5,1},{6,2},{7,3},{8,4},{9,5},{1... | collective-permute-start | bytes 1179656 | tf_op jit(solution)/shard_map/ppermute | solution.py:431
  7.0 19.3 %collective-permute-start.7 = (bf16[256,768]{1,0:T(8,128)(2,1)}, bf16[256,768]{1,0:T(8,128)(2,1)S(1)}, u32[]{:S(2)}, u32[]{:S(2)}) collective-permute-start(bf16[256,768]{1,0:T(8,128)(2,1)} %get-tuple-element.32), channel_id=1, source_target_pairs={{0,1},{1,2},{2,3},{3,4},{4,5},{5,6},{6,7},{7,8},{8,9},{9,10},{10,1... | collective-permute-start | bytes 1179656 | tf_op jit(solution)/shard_map/ppermute | solution.py:431
  10.2 18.7 %collective-permute-start.8 = (bf16[256,768]{1,0:T(8,128)(2,1)}, bf16[256,768]{1,0:T(8,128)(2,1)S(1)}, u32[]{:S(2)}, u32[]{:S(2)}) collective-permute-start(bf16[256,768]{1,0:T(8,128)(2,1)} %get-tuple-element.33), channel_id=1, source_target_pairs={{1,0},{2,1},{3,2},{4,3},{5,4},{6,5},{7,6},{8,7},{9,8},{10,9},{11,1... | collective-permute-start | bytes 1179656 | tf_op jit(solution)/shard_map/ppermute | solution.py:431
  13.0 1.4 %copy-start = (bf16[1024,768]{1,0:T(8,128)(2,1)S(1)}, bf16[1024,768]{1,0:T(8,128)(2,1)}, u32[]{:S(2)}) copy-start(bf16[1024,768]{1,0:T(8,128)(2,1)} %points_ref) | copy-start | bytes 4718596
  14.4 0.7 copy-start.1
  15.1 2.0 %copy-start.2 = (bf16[768,2304]{1,0:T(8,128)(2,1)S(1)}, bf16[768,2304]{1,0:T(8,128)(2,1)}, u32[]{:S(2)}) copy-start(bf16[768,2304]{1,0:T(8,128)(2,1)} %weight_ref.1) | copy-start | bytes 10616836
  17.1 1.3 %copy-start.5 = (bf16[768,768]{1,0:T(8,128)(2,1)S(1)}, bf16[768,768]{1,0:T(8,128)(2,1)}, u32[]{:S(2)}) copy-start(bf16[768,768]{1,0:T(8,128)(2,1)} %wcq_ref.1) | copy-start | bytes 3538948
  18.4 5.3 %copy-start.6 = (bf16[256,768]{1,0:T(8,128)(2,1)S(1)}, bf16[256,768]{1,0:T(8,128)(2,1)}, u32[]{:S(2)}) copy-start(bf16[256,768]{1,0:T(8,128)(2,1)} %get-tuple-element.34.refs_0_) | copy-start | bytes 1179652
  18.4 10.5 %copy-start.3 = (bf16[768,2304]{1,0:T(8,128)(2,1)S(1)}, bf16[768,2304]{1,0:T(8,128)(2,1)}, u32[]{:S(2)}) copy-start(bf16[768,2304]{1,0:T(8,128)(2,1)} %weight_ref.1) | copy-start | bytes 10616836
  18.4 10.5 %copy-start.7 = (s32[8,8]{1,0:T(8,128)S(1)}, s32[8,8]{1,0:T(8,128)}, u32[]{:S(2)}) copy-start(s32[8,8]{1,0:T(8,128)} %ids_ref.1) | copy-start | bytes 772
  18.4 10.5 %copy-start.8 = (s32[8]{0:T(128)S(1)}, s32[8]{0:T(128)}, u32[]{:S(2)}) copy-start(s32[8]{0:T(128)} %count_ref.1) | copy-start | bytes 100
  23.6 18.4 %copy-start.9 = (bf16[1024,3072]{1,0:T(8,128)(2,1)}, bf16[1024,3072]{1,0:T(8,128)(2,1)S(1)}, u32[]{:S(2)}) copy-start(bf16[1024,3072]{1,0:T(8,128)(2,1)S(1)} %shard_map.119.projected_ref.queries_ref) | copy-start | bytes 18874372
  23.7 18.7 %copy-start.4 = (bf16[768,1536]{1,0:T(8,128)(2,1)S(1)}, bf16[768,1536]{1,0:T(8,128)(2,1)}, u32[]{:S(2)}) copy-start(bf16[768,1536]{1,0:T(8,128)(2,1)} %refs_8_.1) | copy-start | bytes 7077892
  23.7 18.4 %collective-permute-start.3 = (bf16[256,768]{1,0:T(8,128)(2,1)S(1)}, bf16[256,768]{1,0:T(8,128)(2,1)S(1)}, u32[]{:S(2)}, u32[]{:S(2)}) collective-permute-start(bf16[256,768]{1,0:T(8,128)(2,1)S(1)} %copy-done.6), channel_id=1, source_target_pairs={{0,8},{1,9},{2,10},{3,11},{4,12},{5,13},{6,14},{7,15},{8,0},{9,1},... | collective-permute-start | bytes 1179656 | tf_op jit(solution)/shard_map/ppermute | solution.py:431
  24.8 17.4 %collective-permute-start.4 = (bf16[256,768]{1,0:T(8,128)(2,1)S(1)}, bf16[256,768]{1,0:T(8,128)(2,1)S(1)}, u32[]{:S(2)}, u32[]{:S(2)}) collective-permute-start(bf16[256,768]{1,0:T(8,128)(2,1)S(1)} %collective-permute-done.1.refs_2_), channel_id=1, source_target_pairs={{0,2},{1,3},{2,0},{3,1},{4,6},{5,7},{6,4},{7,5},{8,10},{9,11},{10,... | collective-permute-start | bytes 1179656 | tf_op jit(solution)/shard_map/ppermute | solution.py:431
  26.2 16.2 %collective-permute-start.5 = (bf16[256,768]{1,0:T(8,128)(2,1)S(1)}, bf16[256,768]{1,0:T(8,128)(2,1)S(1)}, u32[]{:S(2)}, u32[]{:S(2)}) collective-permute-start(bf16[256,768]{1,0:T(8,128)(2,1)S(1)} %collective-permute-done.2.refs_3_), channel_id=1, source_target_pairs={{0,2},{1,3},{2,0},{3,1},{4,6},{5,7},{6,4},{7,5},{8,10},{9,11},{10,... | collective-permute-start | bytes 1179656 | tf_op jit(solution)/shard_map/ppermute | solution.py:431
  26.3 16.1 %collective-permute-start.6 = (bf16[256,768]{1,0:T(8,128)(2,1)S(1)}, bf16[256,768]{1,0:T(8,128)(2,1)S(1)}, u32[]{:S(2)}, u32[]{:S(2)}) collective-permute-start(bf16[256,768]{1,0:T(8,128)(2,1)S(1)} %collective-permute-done.refs_1_), channel_id=1, source_target_pairs={{0,8},{1,9},{2,10},{3,11},{4,12},{5,13},{6,14},{7,15},{8,0},{9,1},... | collective-permute-start | bytes 1179656 | tf_op jit(solution)/shard_map/ppermute | solution.py:431
  42.1 6.7 %copy-start.10 = (bf16[1024,768]{1,0:T(8,128)(2,1)}, bf16[1024,768]{1,0:T(8,128)(2,1)S(1)}, u32[]{:S(2)}) copy-start(bf16[1024,768]{1,0:T(8,128)(2,1)S(1)} %shard_map.120.block_source_ref) | copy-start | bytes 4718596
  48.8 40.9 %collective-permute-start.9 = (bf16[2048,1536]{1,0:T(8,128)(2,1)}, bf16[2048,1536]{1,0:T(8,128)(2,1)}, u32[]{:S(2)}, u32[]{:S(2)}) collective-permute-start(bf16[2048,1536]{1,0:T(8,128)(2,1)} %shard_map.121.keys_ref.values_ref), channel_id=1, source_target_pairs={{0,1},{1,0},{2,3},{3,2},{4,5},{5,4},{6,7},{7,6},{8,9},{9,8},{10,11... | collective-permute-start | bytes 18874376 | tf_op jit(solution)/shard_map/ppermute | solution.py:431
where the time goes:
time: 127 us
  Pallas kernels  98.3 us (77%)
  starting transfers between devices  21.9 us (17%)
  local copies, waits for them, and re-layouts  5.39 us (4%)
    pallas_call x1, Pallas kernels, finish(): pl.pallas_call(final_kernel, out_shape=struct(rows, width), grid_spec=plt...  37 us
    pallas_call x1, Pallas kernels, cross_part(): pl.pallas_call(cross_kernel, out_shape=(state, state), grid=(pairs, rows...  32.7 us
    ppermute x10, starting transfers between devices, permute(): return lax.ppermute(array, 'dom', pairs)  21.9 us
    pallas_call x1, Pallas kernels, block_attention(): pl.pallas_call(block_kernel, out_shape=struct(rows, width), grid_spec=plt...  13.1 us
    pallas_call x1, Pallas kernels, anchor_project(): pl.pallas_call(functools.partial(anchor_kernel, len(parts)), out_shape=st...  6.42 us
    unnamed x22, local copies, waits for them, and re-layouts  5.39 us
    pallas_call x1, Pallas kernels, project(): pl.pallas_call(project_kernel, out_shape=struct(rows, 4 * width), in_spec...  5.23 us
    pallas_call x1, Pallas kernels, pick(): pl.pallas_call(pick_kernel, out_shape=(own, side, side), in_specs=[pl.Blo...  3.84 us
  transfers between devices with their start and end apart: 10, of which 1 were waited for; matrix products, arithmetic and copies ran while one was open for 0% of the time, Pallas kernels for 40%

commit v1 on v0

--- a/solution.py
+++ b/solution.py
@@ -52,25 +52,38 @@
 
 
 def pick_kernel(
-    send_ref, index_ref, gain_ref, source_ref, anchor_ref, prev_ref, next_ref, points_ref, sem
+    send_ref,
+    index_ref,
+    gain_ref,
+    source_ref,
+    anchor_ref,
+    prev_ref,
+    next_ref,
+    out_ref,
+    points_ref,
+    normed_ref,
+    sems,
 ):
-    copy = pltpu.make_async_copy(source_ref, points_ref, sem)
-    copy.start()
     rows = points_ref.shape[0]
+    tile = rows // 4
+    fetch = pltpu.make_async_copy(source_ref, points_ref, sems.at[0])
+    store = pltpu.make_async_copy(normed_ref, out_ref, sems.at[1])
+    fetch.start()
     anchors = index_ref.shape[1]
     slot = lax.broadcasted_iota(jnp.int32, (rows, anchors), 0)
     chosen = jnp.where(slot == index_ref[...], 1.0, 0.0).astype(BF16)
-    copy.wait()
-    picked = lax.dot_general(
-        chosen, points_ref[...], (((0,), (0,)), ((), ())), preferred_element_type=F32
-    )
-    anchor_ref[...] = normed_rows(picked, gain_ref[...])
+    fetch.wait()
+    for at in range(0, rows, tile):
+        normed_ref[at : at + tile, :] = normed_rows(points_ref[at : at + tile, :], gain_ref[...])
+    store.start()
+    anchor_ref[...] = lax.dot_general(
+        chosen, normed_ref[...], (((0,), (0,)), ((), ())), preferred_element_type=F32
+    ).astype(BF16)
     for place in range(HB):
-        for base, out_ref in ((0, prev_ref), (HB, next_ref)):
+        for base, side_ref in ((0, prev_ref), (HB, next_ref)):
             start = pl.multiple_of(send_ref[base + place] * BLK, BLK)
-            out_ref[place * BLK : (place + 1) * BLK, :] = normed_rows(
-                points_ref[pl.ds(start, BLK), :], gain_ref[...]
-            )
+            side_ref[place * BLK : (place + 1) * BLK, :] = normed_ref[pl.ds(start, BLK), :]
+    store.wait()
 
 
 def pick(points, gain, send_blocks, anchor_index):
@@ -80,45 +93,41 @@
     own = struct(anchors, width)
     side = struct(HB * BLK, width)
     vmem = pl.BlockSpec(memory_space=pltpu.VMEM)
+    hbm = pl.BlockSpec(memory_space=pltpu.HBM)
     return pl.pallas_call(
         pick_kernel,
-        out_shape=(own, side, side),
-        in_specs=[
-            pl.BlockSpec(memory_space=pltpu.SMEM),
-            vmem,
-            vmem,
-            pl.BlockSpec(memory_space=pltpu.HBM),
+        out_shape=(own, side, side, struct(rows, width)),
+        in_specs=[pl.BlockSpec(memory_space=pltpu.SMEM), vmem, vmem, hbm],
+        out_specs=(vmem, vmem, vmem, hbm),
+        scratch_shapes=[
+            pltpu.VMEM((rows, width), BF16),
+            pltpu.VMEM((rows, width), BF16),
+            pltpu.SemaphoreType.DMA((2,)),
         ],
-        scratch_shapes=[pltpu.VMEM((rows, width), BF16), pltpu.SemaphoreType.DMA],
         compiler_params=params(WIDE),
-        cost_estimate=cost(2 * anchors * rows * width, 4 * rows * width),
+        cost_estimate=cost(2 * anchors * rows * width, 6 * rows * width),
     )(send_blocks, index, gain, points)
 
 
-def project_kernel(points_ref, gain_ref, wqkv_ref, wcq_ref, out_ref, normed_ref):
-    rows, width = points_ref.shape
-    tile = rows // 4
-    for at in range(0, rows, tile):
-        normed = normed_rows(points_ref[at : at + tile, :], gain_ref[...])
-        normed_ref[at : at + tile, :] = normed
-        out_ref[at : at + tile, :width] = (mm(normed, wqkv_ref[:, :width]) * SCALE).astype(BF16)
-    for at in range(width, 3 * width, width):
-        out_ref[:, at : at + width] = mm(normed_ref[...], wqkv_ref[:, at : at + width]).astype(BF16)
+def project_kernel(normed_ref, wqkv_ref, wcq_ref, out_ref):
+    width = normed_ref.shape[1]
+    for at in range(0, 3 * width, width):
+        made = mm(normed_ref[...], wqkv_ref[:, at : at + width])
+        out_ref[:, at : at + width] = (made * SCALE if at == 0 else made).astype(BF16)
     out_ref[:, 3 * width :] = (mm(normed_ref[...], wcq_ref[...]) * SCALE).astype(BF16)
 
 
-def project(points, gain, w_qkv, w_cross_q):
-    rows, width = points.shape
+def project(normed, w_qkv, w_cross_q):
+    rows, width = normed.shape
     vmem = pl.BlockSpec(memory_space=pltpu.VMEM)
     return pl.pallas_call(
         project_kernel,
         out_shape=struct(rows, 4 * width),
-        in_specs=[vmem] * 4,
+        in_specs=[vmem] * 3,
         out_specs=vmem,
-        scratch_shapes=[pltpu.VMEM((rows, width), BF16)],
         compiler_params=params(24 * 2**20),
         cost_estimate=cost(2 * rows * width * 4 * width, 20 * rows * width),
-    )(points, gain, w_qkv, w_cross_q)
+    )(normed, w_qkv, w_cross_q)
 
 
 def split_heads(rows):
@@ -165,23 +174,28 @@
     out_ref,
     table_ref,
 ):
-    block = pl.program_id(0)
+    width = low_ref.shape[1]
+
+    normed = jnp.concatenate([low_ref[...], high_ref[...]], axis=0)
+    for n in range(2):
+        table_ref[n] = mm(normed, weight_ref[:, (1 + n) * width : (2 + n) * width]).astype(BF16)
+
+    @pl.loop(0, count_ref.shape[0])
+    def _(block):
+        attend_block(block, ids_ref, count_ref, live_ref, projected_ref, table_ref, out_ref)
+
+
+def attend_block(block, ids_ref, count_ref, live_ref, projected_ref, table_ref, out_ref):
     slots = ids_ref.shape[1]
     blocks = count_ref.shape[0]
-    width = low_ref.shape[1]
-
-    @pl.when(block == 0)
-    def _():
-        normed = jnp.concatenate([low_ref[...], high_ref[...]], axis=0)
-        for n in range(2):
-            table_ref[n] = mm(normed, weight_ref[:, (1 + n) * width : (2 + n) * width]).astype(BF16)
-
+    width = out_ref.shape[1]
+    here = pl.ds(pl.multiple_of(block * BLK, BLK), BLK)
     count = count_ref[block]
     pairs = jnp.where(block < live_ref[0], (count + 1) // 2, 0)
 
     @pl.when(pairs == 0)
     def _():
-        out_ref[...] = jnp.zeros_like(out_ref)
+        out_ref[here, :] = jnp.zeros((BLK, width), BF16)
 
     for used in range(1, slots // 2 + 1):
 
@@ -194,7 +208,6 @@
                 received = pl.multiple_of(jnp.maximum(place - blocks, 0) * BLK, BLK)
                 places.append((place < blocks, own, received))
             dropped = jnp.where(count == 2 * used, 0.0, NEG)
-            here = pl.ds(pl.multiple_of(block * BLK, BLK), BLK)
 
             def rows_of(which, part, at):
                 lanes = slice((1 + which) * width + at, (1 + which) * width + at + PAIR)
@@ -221,27 +234,23 @@
                     weigh_wide(jnp.exp2(scores[part] - top), rows_of(1, part, at))
                     for part in range(used)
                 )
-                out_ref[:, at : at + PAIR] = join_heads(total[:, :PAIR] / total[:, PAIR:]).astype(
-                    BF16
-                )
+                out_ref[here, at : at + PAIR] = join_heads(
+                    total[:, :PAIR] / total[:, PAIR:]
+                ).astype(BF16)
 
 
 def block_attention(projected, low, high, w_qkv, ids, counts, live):
     rows = projected.shape[0]
     width = low.shape[1]
     side = low.shape[0]
-    blocks = rows // BLK
     vmem = pl.BlockSpec(memory_space=pltpu.VMEM)
+    smem = pl.BlockSpec(memory_space=pltpu.SMEM)
     return pl.pallas_call(
         block_kernel,
         out_shape=struct(rows, width),
-        grid_spec=pltpu.PrefetchScalarGridSpec(
-            num_scalar_prefetch=3,
-            grid=(blocks,),
-            in_specs=[vmem] * 4,
-            out_specs=pl.BlockSpec((BLK, width), lambda i, *_: (i, 0)),
-            scratch_shapes=[pltpu.VMEM((2, 2 * side, width), BF16)],
-        ),
+        in_specs=[smem] * 3 + [vmem] * 4,
+        out_specs=vmem,
+        scratch_shapes=[pltpu.VMEM((2, 2 * side, width), BF16)],
         compiler_params=params(),
         cost_estimate=cost(16 * rows * 5 * BLK * width, 12 * rows * width, rows * 5 * BLK * 12),
     )(ids, counts, live, projected, low, high, w_qkv)
@@ -445,10 +454,9 @@
     neighbour_count,
     anchor_index,
 ):
-    rows, width = points.shape
     size = lax.axis_size("dom")
     column, ring = 2, 4
-    anchors, to_prev, to_next = pick(points, norm_gain, send_blocks, anchor_index)
+    anchors, to_prev, to_next, normed = pick(points, norm_gain, send_blocks, anchor_index)
 
     def around(array):
         return [permute(array, lambda i, n=n: (i + n * ring) % size) for n in (1, -1, 2)]
@@ -457,8 +465,7 @@
     low = permute(to_next, lambda i: i + 1)
     high = permute(to_prev, lambda i: i - 1)
     rows_here = around(anchors)
-    points, anchors = after(points, anchors)
-    projected = project(points, norm_gain, w_qkv, w_cross_q)
+    projected = project(normed, w_qkv, w_cross_q)
     beside, rows_here[0], rows_here[1], projected = after(
         beside, rows_here[0], rows_here[1], projected
     )

time: 127 us -> 128 us (level)
  the two profiles are of different devices: /device:TPU:23 before, /device:TPU:1 now
where the time goes in v1:
time: 128 us; the launch traced here: 125 us
  Pallas kernels  100 us (78%)
  starting transfers between devices  17.3 us (14%)
  local copies, waits for them, and re-layouts  4.7 us (4%)
  waiting for transfers between devices  1.88 us (1%)
    pallas_call x1, Pallas kernels, finish(): pl.pallas_call(final_kernel, out_shape=struct(rows, width), grid_spec=plt...  37 us
    pallas_call x1, Pallas kernels, cross_part(): pl.pallas_call(cross_kernel, out_shape=(state, state), grid=(pairs, rows...  32.6 us
    ppermute x10, starting transfers between devices, permute(): return lax.ppermute(array, 'dom', pairs)  17.3 us
    pallas_call x1, Pallas kernels, block_attention(): pl.pallas_call(block_kernel, out_shape=struct(rows, width), in_specs=[sme...  13.9 us
    pallas_call x1, Pallas kernels, anchor_project(): pl.pallas_call(functools.partial(anchor_kernel, len(parts)), out_shape=st...  6.42 us
    pallas_call x1, Pallas kernels, pick(): pl.pallas_call(pick_kernel, out_shape=(own, side, side, struct(rows, widt...  5.15 us
    pallas_call x1, Pallas kernels, project(): pl.pallas_call(project_kernel, out_shape=struct(rows, 4 * width), in_spec...  5.04 us
    unnamed x20, local copies, waits for them, and re-layouts  4.7 us
  transfers between devices with their start and end apart: 10, of which 1 were waited for; matrix products, arithmetic and copies ran while one was open for 0% of the time, Pallas kernels for 41%

profile of v1, /device:TPU:1, one launch (start us, length us, event | category | flops | bytes accessed | tf_op | source)
XLA Modules:
  0.0 125.1 jit_solution(16000806725954969059)
XLA Ops:
  0.0 5.2 %shard_map.118 = (bf16[256,768]{1,0:T(8,128)(2,1)}, bf16[256,768]{1,0:T(8,128)(2,1)}, bf16[256,768]{1,0:T(8,128)(2,1)}, bf16[1024,768]{1,0:T(8,128)(2,1)}) custom-call(s32[4]{0:T(128)} %send_ref.1, s32[1,256]{1,0:T(1,128)} %bitcast.1, f32[768]{0:T(1024)} %gain_ref.1, bf16[1024,768]{1,0:T(8,128)(2,1)} %source_ref.1), custom_call_target="tpu_custom_call" | custom-call | flops 402653184 | bytes 4718592 | tf_op jit(solution)/shard_map/pallas_call | solution.py:97
  5.2 2.5 %collective-permute-start = (bf16[256,768]{1,0:T(8,128)(2,1)}, bf16[256,768]{1,0:T(8,128)(2,1)S(1)}, u32[]{:S(2)}, u32[]{:S(2)}) collective-permute-start(bf16[256,768]{1,0:T(8,128)(2,1)} %get-tuple-element.32.refs_0_), channel_id=1, source_target_pairs={{0,2},{1,3},{2,0},{3,1},{4,6},{5,7},{6,4},{7,5},{8,10},{9,11},{10,... | collective-permute-start | bytes 1179656 | tf_op jit(solution)/shard_map/ppermute | solution.py:440
  7.7 1.3 %collective-permute-start.1 = (bf16[256,768]{1,0:T(8,128)(2,1)}, bf16[256,768]{1,0:T(8,128)(2,1)S(1)}, u32[]{:S(2)}, u32[]{:S(2)}) collective-permute-start(bf16[256,768]{1,0:T(8,128)(2,1)} %get-tuple-element.32.refs_0_), channel_id=1, source_target_pairs={{0,4},{1,5},{2,6},{3,7},{4,8},{5,9},{6,10},{7,11},{8,12},{9,13},{1... | collective-permute-start | bytes 1179656 | tf_op jit(solution)/shard_map/ppermute | solution.py:440
  9.0 1.4 %collective-permute-start.2 = (bf16[256,768]{1,0:T(8,128)(2,1)}, bf16[256,768]{1,0:T(8,128)(2,1)S(1)}, u32[]{:S(2)}, u32[]{:S(2)}) collective-permute-start(bf16[256,768]{1,0:T(8,128)(2,1)} %get-tuple-element.32.refs_0_), channel_id=1, source_target_pairs={{0,12},{1,13},{2,14},{3,15},{4,0},{5,1},{6,2},{7,3},{8,4},{9,5},{1... | collective-permute-start | bytes 1179656 | tf_op jit(solution)/shard_map/ppermute | solution.py:440
  10.4 3.0 %collective-permute-start.7 = (bf16[256,768]{1,0:T(8,128)(2,1)}, bf16[256,768]{1,0:T(8,128)(2,1)S(1)}, u32[]{:S(2)}, u32[]{:S(2)}) collective-permute-start(bf16[256,768]{1,0:T(8,128)(2,1)} %get-tuple-element.30), channel_id=1, source_target_pairs={{0,1},{1,2},{2,3},{3,4},{4,5},{5,6},{6,7},{7,8},{8,9},{9,10},{10,1... | collective-permute-start | bytes 1179656 | tf_op jit(solution)/shard_map/ppermute | solution.py:440
  13.5 1.9 %collective-permute-start.8 = (bf16[256,768]{1,0:T(8,128)(2,1)}, bf16[256,768]{1,0:T(8,128)(2,1)S(1)}, u32[]{:S(2)}, u32[]{:S(2)}) collective-permute-start(bf16[256,768]{1,0:T(8,128)(2,1)} %get-tuple-element.31), channel_id=1, source_target_pairs={{1,0},{2,1},{3,2},{4,3},{5,4},{6,5},{7,6},{8,7},{9,8},{10,9},{11,1... | collective-permute-start | bytes 1179656 | tf_op jit(solution)/shard_map/ppermute | solution.py:440
  16.1 0.0 copy-start
  16.1 2.0 %copy-done = bf16[768,2304]{1,0:T(8,128)(2,1)S(1)} copy-done((bf16[768,2304]{1,0:T(8,128)(2,1)S(1)}, bf16[768,2304]{1,0:T(8,128)(2,1)}, u32[]{:S(2)}) %copy-start) | copy-done | bytes 3538968
  18.1 1.4 %copy-done.3 = bf16[1024,768]{1,0:T(8,128)(2,1)S(1)} copy-done((bf16[1024,768]{1,0:T(8,128)(2,1)S(1)}, bf16[1024,768]{1,0:T(8,128)(2,1)}, u32[]{:S(2)}) %copy-start.3) | copy-done | bytes 1572888
  19.5 1.3 %copy-done.4 = bf16[768,768]{1,0:T(8,128)(2,1)S(1)} copy-done((bf16[768,768]{1,0:T(8,128)(2,1)S(1)}, bf16[768,768]{1,0:T(8,128)(2,1)}, u32[]{:S(2)}) %copy-start.4) | copy-done | bytes 1179672
  20.8 5.0 %shard_map.119.projected_ref.queries_ref = bf16[1024,3072]{1,0:T(8,128)(2,1)S(1)} custom-call(bf16[1024,768]{1,0:T(8,128)(2,1)S(1)} %copy-done.3, bf16[768,2304]{1,0:T(8,128)(2,1)S(1)} %copy-done, bf16[768,768]{1,0:T(8,128)(2,1)S(1)} %copy-done.4), custom_call_target="tpu_custom_call" | custom-call | flops 4831838208 | bytes 15728640 | tf_op jit(solution)/shard_map/pallas_call | solution.py:123
  25.8 0.0 copy-start.2
  25.9 2.1 %collective-permute-start.3 = (bf16[256,768]{1,0:T(8,128)(2,1)S(1)}, bf16[256,768]{1,0:T(8,128)(2,1)S(1)}, u32[]{:S(2)}, u32[]{:S(2)}) collective-permute-start(bf16[256,768]{1,0:T(8,128)(2,1)S(1)} %copy-done.5), channel_id=1, source_target_pairs={{0,8},{1,9},{2,10},{3,11},{4,12},{5,13},{6,14},{7,15},{8,0},{9,1},... | collective-permute-start | bytes 1179656 | tf_op jit(solution)/shard_map/ppermute | solution.py:440
  28.0 2.1 %collective-permute-start.4 = (bf16[256,768]{1,0:T(8,128)(2,1)S(1)}, bf16[256,768]{1,0:T(8,128)(2,1)S(1)}, u32[]{:S(2)}, u32[]{:S(2)}) collective-permute-start(bf16[256,768]{1,0:T(8,128)(2,1)S(1)} %collective-permute-done.1.refs_2_), channel_id=1, source_target_pairs={{0,2},{1,3},{2,0},{3,1},{4,6},{5,7},{6,4},{7,5},{8,10},{9,11},{10,... | collective-permute-start | bytes 1179656 | tf_op jit(solution)/shard_map/ppermute | solution.py:440
  30.0 0.1 collective-permute-start.5
  30.1 0.3 collective-permute-start.6
  30.5 0.0 collective-permute-done.8.high_ref
  30.5 13.9 %shard_map.120.block_source_ref = bf16[1024,768]{1,0:T(8,128)(2,1)S(1)} custom-call(s32[8,8]{1,0:T(8,128)S(1)} %copy-done.6, s32[8]{0:T(128)S(1)} %copy-done.7, s32[1]{0:T(128)S(6)} %copy.13.live_ref, bf16[1024,3072]{1,0:T(8,128)(2,1)S(1)} %shard_map.119.projected_ref.queries_ref, bf16[256,768]{1,0:T(8,128)(2,1)S(1)} %collective-permute-done.7.low_ref, ...), custom_call_target="tpu_custom_call" | custom-call | flops 8053063680 | bytes 9437184 | tf_op jit(solution)/shard_map/pallas_call | solution.py:248
  44.4 0.0 collective-permute-done.3.refs_4_
  44.5 1.9 %collective-permute-done.5.refs_6_ = bf16[256,768]{1,0:T(8,128)(2,1)S(1)} collective-permute-done((bf16[256,768]{1,0:T(8,128)(2,1)S(1)}, bf16[256,768]{1,0:T(8,128)(2,1)S(1)}, u32[]{:S(2)}, u32[]{:S(2)}) %collective-permute-start.5) | collective-permute-done | bytes 393248 | tf_op jit(solution)/shard_map/ppermute | solution.py:440
  46.3 6.4 %shard_map.121.keys_ref.values_ref = bf16[2048,1536]{1,0:T(8,128)(2,1)} custom-call(bf16[256,768]{1,0:T(8,128)(2,1)S(1)} %copy-done.5, bf16[256,768]{1,0:T(8,128)(2,1)S(1)} %collective-permute-done.refs_1_, bf16[256,768]{1,0:T(8,128)(2,1)S(1)} %collective-permute-done.1.refs_2_, bf16[256,768]{1,0:T(8,128)(2,1)S(1)} %collective-permute-done.2.refs_3_, ...), custom_call_target="tpu_custom_call" | custom-call | flops 4831838208 | bytes 9437184 | tf_op jit(solution)/shard_map/pallas_call | solution.py:286
  52.8 2.5 %collective-permute-start.9 = (bf16[2048,1536]{1,0:T(8,128)(2,1)}, bf16[2048,1536]{1,0:T(8,128)(2,1)}, u32[]{:S(2)}, u32[]{:S(2)}) collective-permute-start(bf16[2048,1536]{1,0:T(8,128)(2,1)} %shard_map.121.keys_ref.values_ref), channel_id=1, source_target_pairs={{0,1},{1,0},{2,3},{3,2},{4,5},{5,4},{6,7},{7,6},{8,9},{9,8},{10,11... | collective-permute-start | bytes 18874376 | tf_op jit(solution)/shard_map/ppermute | solution.py:440
  55.3 32.6 %shard_map.122 = (f32[1024,768]{1,0:T(8,128)}, f32[1024,768]{1,0:T(8,128)}) custom-call(bf16[1024,3072]{1,0:T(8,128)(2,1)} %copy-done.8, bf16[2048,1536]{1,0:T(8,128)(2,1)} %shard_map.121.keys_ref.values_ref, bf16[2048,1536]{1,0:T(8,128)(2,1)} %shard_map.121.keys_ref.values_ref), custom_call_target="tpu_custom_call" | custom-call | flops 25769803776 | bytes 15728640 | tf_op jit(solution)/shard_map/pallas_call | solution.py:330
  87.9 37.0 %shard_map.123 = bf16[1024,768]{1,0:T(8,128)(2,1)} custom-call(s32[1]{0:T(128)S(6)} %copy.13.live_ref, bf16[1024,3072]{1,0:T(8,128)(2,1)} %copy-done.8, bf16[2048,1536]{1,0:T(8,128)(2,1)} %collective-permute-done.9.keys_ref.values_ref, bf16[2048,1536]{1,0:T(8,128)(2,1)} %collective-permute-done.9.keys_ref.values_ref, ...), custom_call_target="tpu_custom_call" | custom-call | flops 25769803776 | bytes 22020096 | tf_op jit(solution)/shard_map/pallas_call | solution.py:403
  (22 shorter events, 0.0 us)
Async XLA Ops:
  5.2 20.7 %collective-permute-start = (bf16[256,768]{1,0:T(8,128)(2,1)}, bf16[256,768]{1,0:T(8,128)(2,1)S(1)}, u32[]{:S(2)}, u32[]{:S(2)}) collective-permute-start(bf16[256,768]{1,0:T(8,128)(2,1)} %get-tuple-element.32.refs_0_), channel_id=1, source_target_pairs={{0,2},{1,3},{2,0},{3,1},{4,6},{5,7},{6,4},{7,5},{8,10},{9,11},{10,... | collective-permute-start | bytes 1179656 | tf_op jit(solution)/shard_map/ppermute | solution.py:440
  7.7 20.2 %collective-permute-start.1 = (bf16[256,768]{1,0:T(8,128)(2,1)}, bf16[256,768]{1,0:T(8,128)(2,1)S(1)}, u32[]{:S(2)}, u32[]{:S(2)}) collective-permute-start(bf16[256,768]{1,0:T(8,128)(2,1)} %get-tuple-element.32.refs_0_), channel_id=1, source_target_pairs={{0,4},{1,5},{2,6},{3,7},{4,8},{5,9},{6,10},{7,11},{8,12},{9,13},{1... | collective-permute-start | bytes 1179656 | tf_op jit(solution)/shard_map/ppermute | solution.py:440
  9.0 19.0 %collective-permute-start.2 = (bf16[256,768]{1,0:T(8,128)(2,1)}, bf16[256,768]{1,0:T(8,128)(2,1)S(1)}, u32[]{:S(2)}, u32[]{:S(2)}) collective-permute-start(bf16[256,768]{1,0:T(8,128)(2,1)} %get-tuple-element.32.refs_0_), channel_id=1, source_target_pairs={{0,12},{1,13},{2,14},{3,15},{4,0},{5,1},{6,2},{7,3},{8,4},{9,5},{1... | collective-permute-start | bytes 1179656 | tf_op jit(solution)/shard_map/ppermute | solution.py:440
  10.4 19.7 %collective-permute-start.7 = (bf16[256,768]{1,0:T(8,128)(2,1)}, bf16[256,768]{1,0:T(8,128)(2,1)S(1)}, u32[]{:S(2)}, u32[]{:S(2)}) collective-permute-start(bf16[256,768]{1,0:T(8,128)(2,1)} %get-tuple-element.30), channel_id=1, source_target_pairs={{0,1},{1,2},{2,3},{3,4},{4,5},{5,6},{6,7},{7,8},{8,9},{9,10},{10,1... | collective-permute-start | bytes 1179656 | tf_op jit(solution)/shard_map/ppermute | solution.py:440
  13.5 17.0 %collective-permute-start.8 = (bf16[256,768]{1,0:T(8,128)(2,1)}, bf16[256,768]{1,0:T(8,128)(2,1)S(1)}, u32[]{:S(2)}, u32[]{:S(2)}) collective-permute-start(bf16[256,768]{1,0:T(8,128)(2,1)} %get-tuple-element.31), channel_id=1, source_target_pairs={{1,0},{2,1},{3,2},{4,3},{5,4},{6,5},{7,6},{8,7},{9,8},{10,9},{11,1... | collective-permute-start | bytes 1179656 | tf_op jit(solution)/shard_map/ppermute | solution.py:440
  16.1 2.0 %copy-start = (bf16[768,2304]{1,0:T(8,128)(2,1)S(1)}, bf16[768,2304]{1,0:T(8,128)(2,1)}, u32[]{:S(2)}) copy-start(bf16[768,2304]{1,0:T(8,128)(2,1)} %weight_ref.1) | copy-start | bytes 10616836
  18.1 1.4 %copy-start.3 = (bf16[1024,768]{1,0:T(8,128)(2,1)S(1)}, bf16[1024,768]{1,0:T(8,128)(2,1)}, u32[]{:S(2)}) copy-start(bf16[1024,768]{1,0:T(8,128)(2,1)} %get-tuple-element.25.normed_ref) | copy-start | bytes 4718596
  19.5 1.3 %copy-start.4 = (bf16[768,768]{1,0:T(8,128)(2,1)S(1)}, bf16[768,768]{1,0:T(8,128)(2,1)}, u32[]{:S(2)}) copy-start(bf16[768,768]{1,0:T(8,128)(2,1)} %wcq_ref.1) | copy-start | bytes 3538948
  20.8 5.1 %copy-start.5 = (bf16[256,768]{1,0:T(8,128)(2,1)S(1)}, bf16[256,768]{1,0:T(8,128)(2,1)}, u32[]{:S(2)}) copy-start(bf16[256,768]{1,0:T(8,128)(2,1)} %get-tuple-element.32.refs_0_) | copy-start | bytes 1179652
  20.8 9.7 %copy-start.1 = (bf16[768,2304]{1,0:T(8,128)(2,1)S(1)}, bf16[768,2304]{1,0:T(8,128)(2,1)}, u32[]{:S(2)}) copy-start(bf16[768,2304]{1,0:T(8,128)(2,1)} %weight_ref.1) | copy-start | bytes 10616836
  20.8 9.7 %copy-start.6 = (s32[8,8]{1,0:T(8,128)S(1)}, s32[8,8]{1,0:T(8,128)}, u32[]{:S(2)}) copy-start(s32[8,8]{1,0:T(8,128)} %ids_ref.1) | copy-start | bytes 772
  20.8 9.7 %copy-start.7 = (s32[8]{0:T(128)S(1)}, s32[8]{0:T(128)}, u32[]{:S(2)}) copy-start(s32[8]{0:T(128)} %count_ref.1) | copy-start | bytes 100
  25.8 18.6 %copy-start.8 = (bf16[1024,3072]{1,0:T(8,128)(2,1)}, bf16[1024,3072]{1,0:T(8,128)(2,1)S(1)}, u32[]{:S(2)}) copy-start(bf16[1024,3072]{1,0:T(8,128)(2,1)S(1)} %shard_map.119.projected_ref.queries_ref) | copy-start | bytes 18874372
  25.8 20.5 %copy-start.2 = (bf16[768,1536]{1,0:T(8,128)(2,1)S(1)}, bf16[768,1536]{1,0:T(8,128)(2,1)}, u32[]{:S(2)}) copy-start(bf16[768,1536]{1,0:T(8,128)(2,1)} %refs_8_.1) | copy-start | bytes 7077892
  25.9 18.6 %collective-permute-start.3 = (bf16[256,768]{1,0:T(8,128)(2,1)S(1)}, bf16[256,768]{1,0:T(8,128)(2,1)S(1)}, u32[]{:S(2)}, u32[]{:S(2)}) collective-permute-start(bf16[256,768]{1,0:T(8,128)(2,1)S(1)} %copy-done.5), channel_id=1, source_target_pairs={{0,8},{1,9},{2,10},{3,11},{4,12},{5,13},{6,14},{7,15},{8,0},{9,1},... | collective-permute-start | bytes 1179656 | tf_op jit(solution)/shard_map/ppermute | solution.py:440
  28.0 16.5 %collective-permute-start.4 = (bf16[256,768]{1,0:T(8,128)(2,1)S(1)}, bf16[256,768]{1,0:T(8,128)(2,1)S(1)}, u32[]{:S(2)}, u32[]{:S(2)}) collective-permute-start(bf16[256,768]{1,0:T(8,128)(2,1)S(1)} %collective-permute-done.1.refs_2_), channel_id=1, source_target_pairs={{0,2},{1,3},{2,0},{3,1},{4,6},{5,7},{6,4},{7,5},{8,10},{9,11},{10,... | collective-permute-start | bytes 1179656 | tf_op jit(solution)/shard_map/ppermute | solution.py:440
  30.0 16.3 %collective-permute-start.5 = (bf16[256,768]{1,0:T(8,128)(2,1)S(1)}, bf16[256,768]{1,0:T(8,128)(2,1)S(1)}, u32[]{:S(2)}, u32[]{:S(2)}) collective-permute-start(bf16[256,768]{1,0:T(8,128)(2,1)S(1)} %collective-permute-done.2.refs_3_), channel_id=1, source_target_pairs={{0,2},{1,3},{2,0},{3,1},{4,6},{5,7},{6,4},{7,5},{8,10},{9,11},{10,... | collective-permute-start | bytes 1179656 | tf_op jit(solution)/shard_map/ppermute | solution.py:440
  30.1 16.2 %collective-permute-start.6 = (bf16[256,768]{1,0:T(8,128)(2,1)S(1)}, bf16[256,768]{1,0:T(8,128)(2,1)S(1)}, u32[]{:S(2)}, u32[]{:S(2)}) collective-permute-start(bf16[256,768]{1,0:T(8,128)(2,1)S(1)} %collective-permute-done.refs_1_), channel_id=1, source_target_pairs={{0,8},{1,9},{2,10},{3,11},{4,12},{5,13},{6,14},{7,15},{8,0},{9,1},... | collective-permute-start | bytes 1179656 | tf_op jit(solution)/shard_map/ppermute | solution.py:440
  44.4 8.3 %copy-start.9 = (bf16[1024,768]{1,0:T(8,128)(2,1)}, bf16[1024,768]{1,0:T(8,128)(2,1)S(1)}, u32[]{:S(2)}) copy-start(bf16[1024,768]{1,0:T(8,128)(2,1)S(1)} %shard_map.120.block_source_ref) | copy-start | bytes 4718596
  52.8 35.1 %collective-permute-start.9 = (bf16[2048,1536]{1,0:T(8,128)(2,1)}, bf16[2048,1536]{1,0:T(8,128)(2,1)}, u32[]{:S(2)}, u32[]{:S(2)}) collective-permute-start(bf16[2048,1536]{1,0:T(8,128)(2,1)} %shard_map.121.keys_ref.values_ref), channel_id=1, source_target_pairs={{0,1},{1,0},{2,3},{3,2},{4,5},{5,4},{6,7},{7,6},{8,9},{9,8},{10,11... | collective-permute-start | bytes 18874376 | tf_op jit(solution)/shard_map/ppermute | solution.py:440

commit v2 on v0

--- a/solution.py
+++ b/solution.py
@@ -164,48 +164,56 @@
     weight_ref,
     out_ref,
     table_ref,
+    sems,
 ):
-    block = pl.program_id(0)
+    rows = projected_ref.shape[0]
+    width = low_ref.shape[1]
+
+    copies = [
+        pltpu.make_async_copy(
+            projected_ref.at[:, (1 + n) * width : (2 + n) * width],
+            table_ref.at[n, :rows],
+            sems.at[n],
+        )
+        for n in range(2)
+    ]
+    for copy in copies:
+        copy.start()
+    normed = jnp.concatenate([low_ref[...], high_ref[...]], axis=0)
+    for n in range(2):
+        made = mm(normed, weight_ref[:, (1 + n) * width : (2 + n) * width])
+        table_ref[n, rows:, :] = made.astype(BF16)
+    for copy in copies:
+        copy.wait()
+
+    @pl.loop(0, count_ref.shape[0])
+    def _(block):
+        attend_block(block, ids_ref, count_ref, live_ref, projected_ref, table_ref, out_ref)
+
+
+def attend_block(block, ids_ref, count_ref, live_ref, projected_ref, table_ref, out_ref):
     slots = ids_ref.shape[1]
-    blocks = count_ref.shape[0]
-    width = low_ref.shape[1]
-
-    @pl.when(block == 0)
-    def _():
-        normed = jnp.concatenate([low_ref[...], high_ref[...]], axis=0)
-        for n in range(2):
-            table_ref[n] = mm(normed, weight_ref[:, (1 + n) * width : (2 + n) * width]).astype(BF16)
-
+    width = out_ref.shape[1]
+    here = pl.ds(pl.multiple_of(block * BLK, BLK), BLK)
     count = count_ref[block]
     pairs = jnp.where(block < live_ref[0], (count + 1) // 2, 0)
 
     @pl.when(pairs == 0)
     def _():
-        out_ref[...] = jnp.zeros_like(out_ref)
+        out_ref[here, :] = jnp.zeros((BLK, width), BF16)
 
     for used in range(1, slots // 2 + 1):
 
         @pl.when(pairs == used)
         def _(used=used):
-            places = []
-            for n in range(2 * used):
-                place = ids_ref[block, n]
-                own = pl.multiple_of(jnp.minimum(place, blocks - 1) * BLK, BLK)
-                received = pl.multiple_of(jnp.maximum(place - blocks, 0) * BLK, BLK)
-                places.append((place < blocks, own, received))
+            starts = [pl.multiple_of(ids_ref[block, n] * BLK, BLK) for n in range(2 * used)]
             dropped = jnp.where(count == 2 * used, 0.0, NEG)
-            here = pl.ds(pl.multiple_of(block * BLK, BLK), BLK)
 
             def rows_of(which, part, at):
-                lanes = slice((1 + which) * width + at, (1 + which) * width + at + PAIR)
                 return jnp.concatenate(
                     [
-                        jnp.where(
-                            is_own,
-                            projected_ref[pl.ds(own, BLK), lanes],
-                            table_ref[which, pl.ds(received, BLK), at : at + PAIR],
-                        )
-                        for is_own, own, received in places[2 * part : 2 * part + 2]
+                        table_ref[which, pl.ds(start, BLK), at : at + PAIR]
+                        for start in starts[2 * part : 2 * part + 2]
                     ],
                     axis=0,
                 )
@@ -221,27 +229,26 @@
                     weigh_wide(jnp.exp2(scores[part] - top), rows_of(1, part, at))
                     for part in range(used)
                 )
-                out_ref[:, at : at + PAIR] = join_heads(total[:, :PAIR] / total[:, PAIR:]).astype(
-                    BF16
-                )
+                out_ref[here, at : at + PAIR] = join_heads(
+                    total[:, :PAIR] / total[:, PAIR:]
+                ).astype(BF16)
 
 
 def block_attention(projected, low, high, w_qkv, ids, counts, live):
     rows = projected.shape[0]
     width = low.shape[1]
     side = low.shape[0]
-    blocks = rows // BLK
     vmem = pl.BlockSpec(memory_space=pltpu.VMEM)
+    smem = pl.BlockSpec(memory_space=pltpu.SMEM)
     return pl.pallas_call(
         block_kernel,
         out_shape=struct(rows, width),
-        grid_spec=pltpu.PrefetchScalarGridSpec(
-            num_scalar_prefetch=3,
-            grid=(blocks,),
-            in_specs=[vmem] * 4,
-            out_specs=pl.BlockSpec((BLK, width), lambda i, *_: (i, 0)),
-            scratch_shapes=[pltpu.VMEM((2, 2 * side, width), BF16)],
-        ),
+        in_specs=[smem] * 3 + [vmem] * 4,
+        out_specs=vmem,
+        scratch_shapes=[
+            pltpu.VMEM((2, rows + 2 * side, width), BF16),
+            pltpu.SemaphoreType.DMA((2,)),
+        ],
         compiler_params=params(),
         cost_estimate=cost(16 * rows * 5 * BLK * width, 12 * rows * width, rows * 5 * BLK * 12),
     )(ids, counts, live, projected, low, high, w_qkv)

time: 127 us -> 127 us (level)
  the two profiles are of different devices: /device:TPU:23 before, /device:TPU:1 now
where the time goes in v2:
time: 127 us; the launch traced here: 125 us
  Pallas kernels  97.5 us (77%)
  starting transfers between devices  17.4 us (14%)
  local copies, waits for them, and re-layouts  5.39 us (4%)
  waiting for transfers between devices  3.39 us (3%)
    pallas_call x1, Pallas kernels, finish(): pl.pallas_call(final_kernel, out_shape=struct(rows, width), grid_spec=plt...  37 us
    pallas_call x1, Pallas kernels, cross_part(): pl.pallas_call(cross_kernel, out_shape=(state, state), grid=(pairs, rows...  32.7 us
    ppermute x10, starting transfers between devices, permute(): return lax.ppermute(array, 'dom', pairs)  17.4 us
    pallas_call x1, Pallas kernels, block_attention(): pl.pallas_call(block_kernel, out_shape=struct(rows, width), in_specs=[sme...  12.4 us
    pallas_call x1, Pallas kernels, anchor_project(): pl.pallas_call(functools.partial(anchor_kernel, len(parts)), out_shape=st...  6.42 us
    unnamed x22, local copies, waits for them, and re-layouts  5.39 us
    pallas_call x1, Pallas kernels, project(): pl.pallas_call(project_kernel, out_shape=struct(rows, 4 * width), in_spec...  5.23 us
    pallas_call x1, Pallas kernels, pick(): pl.pallas_call(pick_kernel, out_shape=(own, side, side), in_specs=[pl.Blo...  3.83 us
  transfers between devices with their start and end apart: 10, of which 1 were waited for; matrix products, arithmetic and copies ran while one was open for 0% of the time, Pallas kernels for 40%

profile of v2, /device:TPU:1, one launch (start us, length us, event | category | flops | bytes accessed | tf_op | source)
XLA Modules:
  0.0 124.7 jit_solution(2743564083114132552)
XLA Ops:
  0.0 3.8 %shard_map.118 = (bf16[256,768]{1,0:T(8,128)(2,1)}, bf16[256,768]{1,0:T(8,128)(2,1)}, bf16[256,768]{1,0:T(8,128)(2,1)}) custom-call(s32[4]{0:T(128)} %send_ref.1, s32[1,256]{1,0:T(1,128)} %bitcast.1, f32[768]{0:T(1024)} %gain_ref.3, bf16[1024,768]{1,0:T(8,128)(2,1)} %points_ref), custom_call_target="tpu_custom_call" | custom-call | flops 402653184 | bytes 3145728 | tf_op jit(solution)/shard_map/pallas_call | solution.py:83
  3.8 2.5 %collective-permute-start = (bf16[256,768]{1,0:T(8,128)(2,1)}, bf16[256,768]{1,0:T(8,128)(2,1)S(1)}, u32[]{:S(2)}, u32[]{:S(2)}) collective-permute-start(bf16[256,768]{1,0:T(8,128)(2,1)} %get-tuple-element.34.refs_0_), channel_id=1, source_target_pairs={{0,2},{1,3},{2,0},{3,1},{4,6},{5,7},{6,4},{7,5},{8,10},{9,11},{10,... | collective-permute-start | bytes 1179656 | tf_op jit(solution)/shard_map/ppermute | solution.py:438
  6.4 1.3 %collective-permute-start.1 = (bf16[256,768]{1,0:T(8,128)(2,1)}, bf16[256,768]{1,0:T(8,128)(2,1)S(1)}, u32[]{:S(2)}, u32[]{:S(2)}) collective-permute-start(bf16[256,768]{1,0:T(8,128)(2,1)} %get-tuple-element.34.refs_0_), channel_id=1, source_target_pairs={{0,4},{1,5},{2,6},{3,7},{4,8},{5,9},{6,10},{7,11},{8,12},{9,13},{1... | collective-permute-start | bytes 1179656 | tf_op jit(solution)/shard_map/ppermute | solution.py:438
  7.7 1.4 %collective-permute-start.2 = (bf16[256,768]{1,0:T(8,128)(2,1)}, bf16[256,768]{1,0:T(8,128)(2,1)S(1)}, u32[]{:S(2)}, u32[]{:S(2)}) collective-permute-start(bf16[256,768]{1,0:T(8,128)(2,1)} %get-tuple-element.34.refs_0_), channel_id=1, source_target_pairs={{0,12},{1,13},{2,14},{3,15},{4,0},{5,1},{6,2},{7,3},{8,4},{9,5},{1... | collective-permute-start | bytes 1179656 | tf_op jit(solution)/shard_map/ppermute | solution.py:438
  9.1 3.0 %collective-permute-start.7 = (bf16[256,768]{1,0:T(8,128)(2,1)}, bf16[256,768]{1,0:T(8,128)(2,1)S(1)}, u32[]{:S(2)}, u32[]{:S(2)}) collective-permute-start(bf16[256,768]{1,0:T(8,128)(2,1)} %get-tuple-element.32), channel_id=1, source_target_pairs={{0,1},{1,2},{2,3},{3,4},{4,5},{5,6},{6,7},{7,8},{8,9},{9,10},{10,1... | collective-permute-start | bytes 1179656 | tf_op jit(solution)/shard_map/ppermute | solution.py:438
  12.2 1.9 %collective-permute-start.8 = (bf16[256,768]{1,0:T(8,128)(2,1)}, bf16[256,768]{1,0:T(8,128)(2,1)S(1)}, u32[]{:S(2)}, u32[]{:S(2)}) collective-permute-start(bf16[256,768]{1,0:T(8,128)(2,1)} %get-tuple-element.33), channel_id=1, source_target_pairs={{1,0},{2,1},{3,2},{4,3},{5,4},{6,5},{7,6},{8,7},{9,8},{10,9},{11,1... | collective-permute-start | bytes 1179656 | tf_op jit(solution)/shard_map/ppermute | solution.py:438
  14.8 0.0 copy-start
  14.8 1.4 %copy-done = bf16[1024,768]{1,0:T(8,128)(2,1)S(1)} copy-done((bf16[1024,768]{1,0:T(8,128)(2,1)S(1)}, bf16[1024,768]{1,0:T(8,128)(2,1)}, u32[]{:S(2)}) %copy-start) | copy-done | bytes 1572888
  16.2 0.7 copy-done.1
  16.9 2.0 %copy-done.2 = bf16[768,2304]{1,0:T(8,128)(2,1)S(1)} copy-done((bf16[768,2304]{1,0:T(8,128)(2,1)S(1)}, bf16[768,2304]{1,0:T(8,128)(2,1)}, u32[]{:S(2)}) %copy-start.2) | copy-done | bytes 3538968
  18.9 1.3 %copy-done.5 = bf16[768,768]{1,0:T(8,128)(2,1)S(1)} copy-done((bf16[768,768]{1,0:T(8,128)(2,1)S(1)}, bf16[768,768]{1,0:T(8,128)(2,1)}, u32[]{:S(2)}) %copy-start.5) | copy-done | bytes 1179672
  20.1 5.2 %shard_map.119.projected_ref.queries_ref = bf16[1024,3072]{1,0:T(8,128)(2,1)S(1)} custom-call(bf16[1024,768]{1,0:T(8,128)(2,1)S(1)} %copy-done, f32[768]{0:T(1024)S(1)} %copy-done.1, bf16[768,2304]{1,0:T(8,128)(2,1)S(1)} %copy-done.2, bf16[768,768]{1,0:T(8,128)(2,1)S(1)} %copy-done.5), custom_call_target="tpu_custom_call" | custom-call | flops 4831838208 | bytes 15728640 | tf_op jit(solution)/shard_map/pallas_call | solution.py:113
  25.4 0.0 copy-start.4
  25.4 2.1 %collective-permute-start.3 = (bf16[256,768]{1,0:T(8,128)(2,1)S(1)}, bf16[256,768]{1,0:T(8,128)(2,1)S(1)}, u32[]{:S(2)}, u32[]{:S(2)}) collective-permute-start(bf16[256,768]{1,0:T(8,128)(2,1)S(1)} %copy-done.6), channel_id=1, source_target_pairs={{0,8},{1,9},{2,10},{3,11},{4,12},{5,13},{6,14},{7,15},{8,0},{9,1},... | collective-permute-start | bytes 1179656 | tf_op jit(solution)/shard_map/ppermute | solution.py:438
  27.5 0.0 collective-permute-done.1.refs_2_
  27.5 2.1 %collective-permute-start.4 = (bf16[256,768]{1,0:T(8,128)(2,1)S(1)}, bf16[256,768]{1,0:T(8,128)(2,1)S(1)}, u32[]{:S(2)}, u32[]{:S(2)}) collective-permute-start(bf16[256,768]{1,0:T(8,128)(2,1)S(1)} %collective-permute-done.1.refs_2_), channel_id=1, source_target_pairs={{0,2},{1,3},{2,0},{3,1},{4,6},{5,7},{6,4},{7,5},{8,10},{9,11},{10,... | collective-permute-start | bytes 1179656 | tf_op jit(solution)/shard_map/ppermute | solution.py:438
  29.6 0.1 collective-permute-start.5
  29.7 0.3 collective-permute-start.6
  30.0 12.4 %shard_map.120.block_source_ref = bf16[1024,768]{1,0:T(8,128)(2,1)S(1)} custom-call(s32[8,8]{1,0:T(8,128)S(1)} %copy-done.7, s32[8]{0:T(128)S(1)} %copy-done.8, s32[1]{0:T(128)S(6)} %copy.13.live_ref, bf16[1024,3072]{1,0:T(8,128)(2,1)S(1)} %shard_map.119.projected_ref.queries_ref, bf16[256,768]{1,0:T(8,128)(2,1)S(1)} %collective-permute-done.7.low_ref, ...), custom_call_target="tpu_custom_call" | custom-call | flops 8053063680 | bytes 9437184 | tf_op jit(solution)/shard_map/pallas_call | solution.py:243
  42.5 3.4 %collective-permute-done.5.refs_6_ = bf16[256,768]{1,0:T(8,128)(2,1)S(1)} collective-permute-done((bf16[256,768]{1,0:T(8,128)(2,1)S(1)}, bf16[256,768]{1,0:T(8,128)(2,1)S(1)}, u32[]{:S(2)}, u32[]{:S(2)}) %collective-permute-start.5) | collective-permute-done | bytes 393248 | tf_op jit(solution)/shard_map/ppermute | solution.py:438
  45.9 6.4 %shard_map.121.keys_ref.values_ref = bf16[2048,1536]{1,0:T(8,128)(2,1)} custom-call(bf16[256,768]{1,0:T(8,128)(2,1)S(1)} %copy-done.6, bf16[256,768]{1,0:T(8,128)(2,1)S(1)} %collective-permute-done.refs_1_, bf16[256,768]{1,0:T(8,128)(2,1)S(1)} %collective-permute-done.1.refs_2_, bf16[256,768]{1,0:T(8,128)(2,1)S(1)} %collective-permute-done.2.refs_3_, ...), custom_call_target="tpu_custom_call" | custom-call | flops 4831838208 | bytes 9437184 | tf_op jit(solution)/shard_map/pallas_call | solution.py:284
  52.3 2.5 %collective-permute-start.9 = (bf16[2048,1536]{1,0:T(8,128)(2,1)}, bf16[2048,1536]{1,0:T(8,128)(2,1)}, u32[]{:S(2)}, u32[]{:S(2)}) collective-permute-start(bf16[2048,1536]{1,0:T(8,128)(2,1)} %shard_map.121.keys_ref.values_ref), channel_id=1, source_target_pairs={{0,1},{1,0},{2,3},{3,2},{4,5},{5,4},{6,7},{7,6},{8,9},{9,8},{10,11... | collective-permute-start | bytes 18874376 | tf_op jit(solution)/shard_map/ppermute | solution.py:438
  54.8 32.7 %shard_map.122 = (f32[1024,768]{1,0:T(8,128)}, f32[1024,768]{1,0:T(8,128)}) custom-call(bf16[1024,3072]{1,0:T(8,128)(2,1)} %copy-done.9, bf16[2048,1536]{1,0:T(8,128)(2,1)} %shard_map.121.keys_ref.values_ref, bf16[2048,1536]{1,0:T(8,128)(2,1)} %shard_map.121.keys_ref.values_ref), custom_call_target="tpu_custom_call" | custom-call | flops 25769803776 | bytes 15728640 | tf_op jit(solution)/shard_map/pallas_call | solution.py:328
  87.5 37.0 %shard_map.123 = bf16[1024,768]{1,0:T(8,128)(2,1)} custom-call(s32[1]{0:T(128)S(6)} %copy.13.live_ref, bf16[1024,3072]{1,0:T(8,128)(2,1)} %copy-done.9, bf16[2048,1536]{1,0:T(8,128)(2,1)} %collective-permute-done.9.keys_ref.values_ref, bf16[2048,1536]{1,0:T(8,128)(2,1)} %collective-permute-done.9.keys_ref.values_ref, ...), custom_call_target="tpu_custom_call" | custom-call | flops 25769803776 | bytes 22020096 | tf_op jit(solution)/shard_map/pallas_call | solution.py:401
  (24 shorter events, 0.1 us)
Async XLA Ops:
  3.8 21.6 %collective-permute-start = (bf16[256,768]{1,0:T(8,128)(2,1)}, bf16[256,768]{1,0:T(8,128)(2,1)S(1)}, u32[]{:S(2)}, u32[]{:S(2)}) collective-permute-start(bf16[256,768]{1,0:T(8,128)(2,1)} %get-tuple-element.34.refs_0_), channel_id=1, source_target_pairs={{0,2},{1,3},{2,0},{3,1},{4,6},{5,7},{6,4},{7,5},{8,10},{9,11},{10,... | collective-permute-start | bytes 1179656 | tf_op jit(solution)/shard_map/ppermute | solution.py:438
  6.4 21.1 %collective-permute-start.1 = (bf16[256,768]{1,0:T(8,128)(2,1)}, bf16[256,768]{1,0:T(8,128)(2,1)S(1)}, u32[]{:S(2)}, u32[]{:S(2)}) collective-permute-start(bf16[256,768]{1,0:T(8,128)(2,1)} %get-tuple-element.34.refs_0_), channel_id=1, source_target_pairs={{0,4},{1,5},{2,6},{3,7},{4,8},{5,9},{6,10},{7,11},{8,12},{9,13},{1... | collective-permute-start | bytes 1179656 | tf_op jit(solution)/shard_map/ppermute | solution.py:438
  7.7 19.8 %collective-permute-start.2 = (bf16[256,768]{1,0:T(8,128)(2,1)}, bf16[256,768]{1,0:T(8,128)(2,1)S(1)}, u32[]{:S(2)}, u32[]{:S(2)}) collective-permute-start(bf16[256,768]{1,0:T(8,128)(2,1)} %get-tuple-element.34.refs_0_), channel_id=1, source_target_pairs={{0,12},{1,13},{2,14},{3,15},{4,0},{5,1},{6,2},{7,3},{8,4},{9,5},{1... | collective-permute-start | bytes 1179656 | tf_op jit(solution)/shard_map/ppermute | solution.py:438
  9.1 20.5 %collective-permute-start.7 = (bf16[256,768]{1,0:T(8,128)(2,1)}, bf16[256,768]{1,0:T(8,128)(2,1)S(1)}, u32[]{:S(2)}, u32[]{:S(2)}) collective-permute-start(bf16[256,768]{1,0:T(8,128)(2,1)} %get-tuple-element.32), channel_id=1, source_target_pairs={{0,1},{1,2},{2,3},{3,4},{4,5},{5,6},{6,7},{7,8},{8,9},{9,10},{10,1... | collective-permute-start | bytes 1179656 | tf_op jit(solution)/shard_map/ppermute | solution.py:438
  12.2 17.9 %collective-permute-start.8 = (bf16[256,768]{1,0:T(8,128)(2,1)}, bf16[256,768]{1,0:T(8,128)(2,1)S(1)}, u32[]{:S(2)}, u32[]{:S(2)}) collective-permute-start(bf16[256,768]{1,0:T(8,128)(2,1)} %get-tuple-element.33), channel_id=1, source_target_pairs={{1,0},{2,1},{3,2},{4,3},{5,4},{6,5},{7,6},{8,7},{9,8},{10,9},{11,1... | collective-permute-start | bytes 1179656 | tf_op jit(solution)/shard_map/ppermute | solution.py:438
  14.8 1.4 %copy-start = (bf16[1024,768]{1,0:T(8,128)(2,1)S(1)}, bf16[1024,768]{1,0:T(8,128)(2,1)}, u32[]{:S(2)}) copy-start(bf16[1024,768]{1,0:T(8,128)(2,1)} %points_ref) | copy-start | bytes 4718596
  16.2 0.7 copy-start.1
  16.8 2.0 %copy-start.2 = (bf16[768,2304]{1,0:T(8,128)(2,1)S(1)}, bf16[768,2304]{1,0:T(8,128)(2,1)}, u32[]{:S(2)}) copy-start(bf16[768,2304]{1,0:T(8,128)(2,1)} %weight_ref.1) | copy-start | bytes 10616836
  18.9 1.3 %copy-start.5 = (bf16[768,768]{1,0:T(8,128)(2,1)S(1)}, bf16[768,768]{1,0:T(8,128)(2,1)}, u32[]{:S(2)}) copy-start(bf16[768,768]{1,0:T(8,128)(2,1)} %wcq_ref.1) | copy-start | bytes 3538948
  20.1 5.3 %copy-start.6 = (bf16[256,768]{1,0:T(8,128)(2,1)S(1)}, bf16[256,768]{1,0:T(8,128)(2,1)}, u32[]{:S(2)}) copy-start(bf16[256,768]{1,0:T(8,128)(2,1)} %get-tuple-element.34.refs_0_) | copy-start | bytes 1179652
  20.1 9.9 %copy-start.3 = (bf16[768,2304]{1,0:T(8,128)(2,1)S(1)}, bf16[768,2304]{1,0:T(8,128)(2,1)}, u32[]{:S(2)}) copy-start(bf16[768,2304]{1,0:T(8,128)(2,1)} %weight_ref.1) | copy-start | bytes 10616836
  20.1 9.9 %copy-start.7 = (s32[8,8]{1,0:T(8,128)S(1)}, s32[8,8]{1,0:T(8,128)}, u32[]{:S(2)}) copy-start(s32[8,8]{1,0:T(8,128)} %ids_ref.1) | copy-start | bytes 772
  20.1 9.9 %copy-start.8 = (s32[8]{0:T(128)S(1)}, s32[8]{0:T(128)}, u32[]{:S(2)}) copy-start(s32[8]{0:T(128)} %count_ref.1) | copy-start | bytes 100
  25.4 17.1 %copy-start.9 = (bf16[1024,3072]{1,0:T(8,128)(2,1)}, bf16[1024,3072]{1,0:T(8,128)(2,1)S(1)}, u32[]{:S(2)}) copy-start(bf16[1024,3072]{1,0:T(8,128)(2,1)S(1)} %shard_map.119.projected_ref.queries_ref) | copy-start | bytes 18874372
  25.4 20.5 %copy-start.4 = (bf16[768,1536]{1,0:T(8,128)(2,1)S(1)}, bf16[768,1536]{1,0:T(8,128)(2,1)}, u32[]{:S(2)}) copy-start(bf16[768,1536]{1,0:T(8,128)(2,1)} %refs_8_.1) | copy-start | bytes 7077892
  25.4 17.1 %collective-permute-start.3 = (bf16[256,768]{1,0:T(8,128)(2,1)S(1)}, bf16[256,768]{1,0:T(8,128)(2,1)S(1)}, u32[]{:S(2)}, u32[]{:S(2)}) collective-permute-start(bf16[256,768]{1,0:T(8,128)(2,1)S(1)} %copy-done.6), channel_id=1, source_target_pairs={{0,8},{1,9},{2,10},{3,11},{4,12},{5,13},{6,14},{7,15},{8,0},{9,1},... | collective-permute-start | bytes 1179656 | tf_op jit(solution)/shard_map/ppermute | solution.py:438
  27.5 15.0 %collective-permute-start.4 = (bf16[256,768]{1,0:T(8,128)(2,1)S(1)}, bf16[256,768]{1,0:T(8,128)(2,1)S(1)}, u32[]{:S(2)}, u32[]{:S(2)}) collective-permute-start(bf16[256,768]{1,0:T(8,128)(2,1)S(1)} %collective-permute-done.1.refs_2_), channel_id=1, source_target_pairs={{0,2},{1,3},{2,0},{3,1},{4,6},{5,7},{6,4},{7,5},{8,10},{9,11},{10,... | collective-permute-start | bytes 1179656 | tf_op jit(solution)/shard_map/ppermute | solution.py:438
  29.6 16.3 %collective-permute-start.5 = (bf16[256,768]{1,0:T(8,128)(2,1)S(1)}, bf16[256,768]{1,0:T(8,128)(2,1)S(1)}, u32[]{:S(2)}, u32[]{:S(2)}) collective-permute-start(bf16[256,768]{1,0:T(8,128)(2,1)S(1)} %collective-permute-done.2.refs_3_), channel_id=1, source_target_pairs={{0,2},{1,3},{2,0},{3,1},{4,6},{5,7},{6,4},{7,5},{8,10},{9,11},{10,... | collective-permute-start | bytes 1179656 | tf_op jit(solution)/shard_map/ppermute | solution.py:438
  29.7 16.2 %collective-permute-start.6 = (bf16[256,768]{1,0:T(8,128)(2,1)S(1)}, bf16[256,768]{1,0:T(8,128)(2,1)S(1)}, u32[]{:S(2)}, u32[]{:S(2)}) collective-permute-start(bf16[256,768]{1,0:T(8,128)(2,1)S(1)} %collective-permute-done.refs_1_), channel_id=1, source_target_pairs={{0,8},{1,9},{2,10},{3,11},{4,12},{5,13},{6,14},{7,15},{8,0},{9,1},... | collective-permute-start | bytes 1179656 | tf_op jit(solution)/shard_map/ppermute | solution.py:438
  42.5 9.8 %copy-start.10 = (bf16[1024,768]{1,0:T(8,128)(2,1)}, bf16[1024,768]{1,0:T(8,128)(2,1)S(1)}, u32[]{:S(2)}) copy-start(bf16[1024,768]{1,0:T(8,128)(2,1)S(1)} %shard_map.120.block_source_ref) | copy-start | bytes 4718596
  52.3 35.2 %collective-permute-start.9 = (bf16[2048,1536]{1,0:T(8,128)(2,1)}, bf16[2048,1536]{1,0:T(8,128)(2,1)}, u32[]{:S(2)}, u32[]{:S(2)}) collective-permute-start(bf16[2048,1536]{1,0:T(8,128)(2,1)} %shard_map.121.keys_ref.values_ref), channel_id=1, source_target_pairs={{0,1},{1,0},{2,3},{3,2},{4,5},{5,4},{6,7},{7,6},{8,9},{9,8},{10,11... | collective-permute-start | bytes 18874376 | tf_op jit(solution)/shard_map/ppermute | solution.py:438
